TPU v7x, 256 devices: a whole 4x4x8 slice. The times are simulated.
256 devices in a mesh: modes: 8 (over y, core), mesh: 32 (over z, x).
Axes of the slice: x: 4, y: 4, z: 8, core: 2. Of those that a mesh axis runs over, the one named last changes fastest.
Arguments:
- velocity: float32 [3, 128, 7, 7, 4096], P(None, 'modes', None, None, 'mesh'), may hold values from -30 to 30
- element_slot: int32 [4096], P('mesh'), may hold values from 0 to 127, as said below
Outputs:
- advanced: float32 [3, 128, 7, 7, 4096], P(None, 'modes', None, None, 'mesh')
Inputs may be any that keep to these rules, and one draw needn't show every extreme that they name: `element_slot`: each aligned block of 128 entries is a permutation of 0 to 127.
All inputs are finite; a program needn't handle non-finite values.
Results may differ from a plain program's by a relative error of at most 0.0003.
Values sent between devices are 32-bit elements; how exact they have to be, the bound alone decides.
A program may use at most 192 MiB of HBM per device.

v0:
```python
import jax
import jax.numpy as jnp
import numpy as np
from jax import lax
from jax.sharding import PartitionSpec as P

EY = 16
ITERS = 3


PRECISE = lax.Precision.HIGHEST
SIGMA_BASE = 8.0
SPAN_WAVE = 0.25
STEP_TIME = 0.01


def with_halo(value, sides, width):
    for axis, dim in sides:
        count, length = (lax.axis_size(axis), value.shape[dim])
        up = [(i, (i + 1) % count) for i in range(count - 1)]
        down = [(j, i) for i, j in up]
        last = lax.slice_in_dim(value, length - width, length, axis=dim)
        leading = lax.slice_in_dim(value, 0, width, axis=dim)
        before = lax.ppermute(last, axis, up)
        after = lax.ppermute(leading, axis, down)
        value = jnp.concatenate([before, value, after], axis=dim)
    return value


def gll_tables():
    inner_point = np.sqrt((5.0 - 2.0 * np.sqrt(5.0 / 3.0)) / 11.0)
    outer_point = np.sqrt((5.0 + 2.0 * np.sqrt(5.0 / 3.0)) / 11.0)
    points = np.array([-1.0, -outer_point, -inner_point, 0.0, inner_point, outer_point, 1.0])
    legendre_prev = points * 0.0 + 1.0
    legendre_now = points.copy()
    for degree in range(1, points.shape[0] - 1):
        legendre_next = ((2 * degree + 1) * points * legendre_now - degree * legendre_prev) / (
            degree + 1
        )
        legendre_prev = legendre_now
        legendre_now = legendre_next
    order_value = points.shape[0] - 1
    quadrature = 2.0 / (order_value * (order_value + 1) * legendre_now**2)
    counter = np.arange(points.shape[0])
    same_node = counter[:, None] == counter[None, :]
    distances = np.where(same_node, 1.0, points[:, None] - points[None, :])
    barycentric = 1.0 / np.prod(distances, axis=1)
    off_diagonal = np.where(same_node, 0.0, barycentric[None, :] / barycentric[:, None] / distances)
    derivative = np.where(same_node, -np.sum(off_diagonal, axis=1)[:, None], off_diagonal)
    stiffness = derivative.T @ (quadrature[:, None] * derivative)
    return (
        jnp.asarray(quadrature, jnp.float32),
        jnp.asarray(derivative, jnp.float32),
        jnp.asarray(stiffness, jnp.float32),
    )


def fourier_tables(coeff_total):
    half_count = coeff_total // 2
    planes = np.arange(coeff_total) * 2.0 * np.pi / coeff_total
    numbers = np.arange(coeff_total)
    wavenumber = np.where(numbers <= half_count, numbers, numbers - half_count)
    cosine_mask = (numbers <= half_count)[None, :]
    phase = planes[:, None] * wavenumber[None, :]
    inverse = np.where(cosine_mask, np.cos(phase), np.sin(phase))
    slope = SPAN_WAVE * wavenumber[None, :] * np.where(cosine_mask, -np.sin(phase), np.cos(phase))
    normaliser = np.where(
        (numbers == 0) | (numbers == half_count), 1.0 / coeff_total, 2.0 / coeff_total
    )
    forward = normaliser[:, None] * inverse.T
    return (
        jnp.asarray(inverse, jnp.float32),
        jnp.asarray(slope, jnp.float32),
        jnp.asarray(forward, jnp.float32),
    )


def transport(physical, stream_slope, cross_slope, span_slope, forward):
    product = -(
        physical[0:1] * stream_slope + physical[1:2] * cross_slope + physical[2:3] * span_slope
    )
    return jnp.einsum("cp,fp...->fc...", forward, product, precision=PRECISE)


def nonlinear(values, inverse, slope, forward, derivative):
    physical = jnp.einsum("pc,fc...->fp...", inverse, values, precision=PRECISE)
    span_slope = jnp.einsum("pc,fc...->fp...", slope, values, precision=PRECISE)
    stream_slope = 2.0 * jnp.einsum("ia,fpab...->fpib...", derivative, physical, precision=PRECISE)
    cross_slope = 2.0 * jnp.einsum("jb,fpab...->fpaj...", derivative, physical, precision=PRECISE)
    return transport(physical, stream_slope, cross_slope, span_slope, forward)


def operate(values, helmholtz, stiffness, quadrature):
    stream_part = (
        jnp.einsum("ia,sajn->sijn", stiffness, values, precision=PRECISE)
        * quadrature[None, None, :, None]
    )
    cross_part = (
        jnp.einsum("jb,sibn->sijn", stiffness, values, precision=PRECISE)
        * quadrature[None, :, None, None]
    )
    mass_diag = 0.25 * quadrature[:, None] * quadrature[None, :]
    return (
        stream_part
        + cross_part
        + helmholtz[:, None, None, None] * mass_diag[None, :, :, None] * values
    )


def assemble_with(element_values, row_count, prior_face, next_face):
    left_face = element_values[:, 0]
    right_face = element_values[:, -1]
    from_prior = jnp.concatenate([prior_face, right_face[..., :-row_count]], axis=-1)
    from_next = jnp.concatenate([left_face[..., row_count:], next_face], axis=-1)
    element_values = jnp.concatenate(
        [
            (left_face + from_prior)[:, None],
            element_values[:, 1:-1],
            (right_face + from_next)[:, None],
        ],
        axis=1,
    )
    bottom_face = element_values[:, :, 0]
    top_face = element_values[:, :, -1]
    position = jnp.arange(element_values.shape[-1]) % row_count
    zero_column = jnp.zeros_like(bottom_face[..., :1])
    from_above = jnp.where(
        position != row_count - 1,
        jnp.concatenate([bottom_face[..., 1:], zero_column], axis=-1),
        0.0,
    )
    from_below = jnp.where(
        position != 0, jnp.concatenate([zero_column, top_face[..., :-1]], axis=-1), 0.0
    )
    return jnp.concatenate(
        [
            (bottom_face + from_below)[:, :, None],
            element_values[:, :, 1:-1],
            (top_face + from_above)[:, :, None],
        ],
        axis=2,
    )


def assemble(element_values, row_count):
    face_pair = jnp.stack(
        [element_values[:, 0, :, :row_count], element_values[:, -1, :, -row_count:]], axis=0
    )
    extended = with_halo(face_pair, (("mesh", 0),), 1)
    return assemble_with(element_values, row_count, extended[0], extended[-1])


def boundary_tables(element_count, row_count, first_column, column_total):
    column = first_column + jnp.arange(element_count) // row_count
    row_index = jnp.arange(element_count) % row_count
    node_index = jnp.arange(7)
    west_side = (node_index == 0)[:, None, None]
    east_side = (node_index == 6)[:, None, None]
    south_side = (node_index == 0)[None, :, None]
    north_side = (node_index == 6)[None, :, None]
    fixed_node = (
        south_side & (row_index == 0)
        | north_side & (row_index == row_count - 1)
        | west_side & (column == 0)
    )
    dirichlet_keep = jnp.where(fixed_node, 0.0, 1.0)
    shared_horizontal = west_side & (column > 0) | east_side & (column < column_total - 1)
    shared_vertical = south_side & (row_index > 0) | north_side & (row_index < row_count - 1)
    weight = 1.0 / (jnp.where(shared_horizontal, 2.0, 1.0) * jnp.where(shared_vertical, 2.0, 1.0))
    return (dirichlet_keep, weight)


def shards(velocity, element_slot):
    groups = lax.axis_size("modes")
    local_coeffs = velocity.shape[1]
    coeff_total = local_coeffs * groups
    element_count = element_slot.shape[0]
    column_count = element_count // EY
    slice_size = element_count // groups
    quadrature, derivative, stiffness = gll_tables()
    inverse, slope, forward = fourier_tables(coeff_total)
    grid_field = jnp.take(velocity, element_slot, axis=4)
    outgoing = grid_field.reshape(3, local_coeffs, 7, 7, groups, slice_size)
    result = nonlinear(
        lax.all_to_all(outgoing, "modes", split_axis=4, concat_axis=1, tiled=True),
        inverse,
        slope,
        forward,
        derivative,
    )
    arriving = lax.all_to_all(result, "modes", split_axis=1, concat_axis=4, tiled=True)
    nonlinear_modes = arriving.reshape(3, local_coeffs, 7, 7, element_count)
    mass_diag = 0.25 * quadrature[:, None] * quadrature[None, :]
    source = (
        mass_diag[:, :, None] * (SIGMA_BASE * grid_field + STEP_TIME * nonlinear_modes)
    ).reshape(3 * local_coeffs, 7, 7, element_count)
    numbers = lax.axis_index("modes") * local_coeffs + jnp.arange(local_coeffs)
    half_count = coeff_total // 2
    wavenumber = jnp.where(numbers <= half_count, numbers, numbers - half_count).astype(jnp.float32)
    helmholtz = jnp.tile(SIGMA_BASE + (SPAN_WAVE * wavenumber) ** 2, 3)
    dirichlet_keep, weight = boundary_tables(
        element_count,
        EY,
        lax.axis_index("mesh") * column_count,
        column_count * lax.axis_size("mesh"),
    )

    def weighted_inner(left_values, right_values):
        return jnp.sum(left_values * right_values * weight, axis=(1, 2, 3))

    def squares(values):
        return lax.psum(weighted_inner(values, values), "mesh")

    def expand_rows(vector):
        return vector[:, None, None, None]

    residual = dirichlet_keep * assemble(source, EY)
    solution = jnp.zeros_like(residual)
    direction = residual
    norm_now = squares(residual)
    for iteration in range(ITERS):
        applied = dirichlet_keep * assemble(
            operate(direction, helmholtz, stiffness, quadrature), EY
        )
        step_size = norm_now / lax.psum(weighted_inner(direction, applied), "mesh")
        solution = solution + expand_rows(step_size) * direction
        residual = residual - expand_rows(step_size) * applied
        if iteration + 1 < ITERS:
            norm_next = squares(residual)
            direction = residual + expand_rows(norm_next / norm_now) * direction
            norm_now = norm_next
    return solution.reshape(3, local_coeffs, 7, 7, element_count)


def solution(mesh):
    placed = (P(None, "modes", None, None, "mesh"), P("mesh"))
    return jax.shard_map(
        shards,
        mesh=mesh,
        in_specs=placed,
        out_specs=P(None, "modes", None, None, "mesh"),
        check_vma=False,
    )
```

profile of v0, /device:TPU:128, one launch (start us, length us, event | category | flops | bytes accessed | tf_op | source)
XLA Modules:
  0.0 712.4 jit_solution(15140324220610625539)
XLA Ops:
  1.4 7.8 %copy.533 = f32[3,16,7,7,128]{1,3,4,2,0:T(8,128)} copy(f32[3,16,7,7,128]{4,1,3,2,0:T(8,128)} %param.8) | data formatting | bytes 2408448 | tf_op args[0]
  9.2 10.3 %gather_fusion = f32[128,3,16,7,7]{2,4,3,1,0:T(8,128)} fusion(f32[3,16,7,7,128]{1,3,4,2,0:T(8,128)} %copy.533, s32[1024]{0:T(1024)S(1)} %pad_clamp_fusion), kind=kCustom, calls=%fused_computation | custom fusion | bytes 2408960 | tf_op jit(solution)/shard_map/jit(_take)/gather | solution.py:182
  19.5 10.2 %fusion.51 = f32[8,3,7,7,16,16]{5,4,3,2,1,0:T(8,128)} fusion(f32[3,16,7,7,8,16]{1,3,2,0,5,4:T(8,128)} %bitcast.242, pred[8,16]{1,0:T(8,128)(4,1)S(1)} %broadcast_in_dim.156), kind=kLoop, calls=%fused_computation.177 | loop fusion | flops 301056 | bytes 2408576
  29.7 8.6 %reshape.474 = f32[8,1,37632]{2,1,0:T(1,128)} reshape(f32[8,3,7,7,16,16]{5,4,3,2,1,0:T(8,128)} %fusion.51) | data formatting | bytes 2408448
  38.3 4.9 all-to-all-start
  43.5 16.9 %all-to-all-done = f32[8,1,37632]{2,1,0:T(1,128)S(1)} async-done(((f32[8,1,37632]{2,1,0:T(1,128)}), f32[8,1,37632]{2,1,0:T(1,128)S(1)}, u32[]{:S(2)}, u32[]{:S(2)}) %all-to-all-start) | async-done | bytes 1204256 | tf_op jit(solution)/shard_map/all_to_all | solution.py:185
  64.6 6.7 reshape.475
  71.3 4.4 bitcast_bitcast_fusion
  75.7 8.5 %copy.536 = f32[3,8,16,7,7,1,16]{2,1,6,4,3,0,5:T(8,128)} copy(f32[3,8,16,7,7,1,16]{2,6,4,3,0,1,5:T(8,128)S(1)} %bitcast_bitcast_fusion) | data formatting | bytes 2408448 | tf_op jit(solution)/shard_map/all_to_all | solution.py:185
  84.2 6.3 reshape.457
  99.3 18.7 %copy.545 = f32[3,128,7,7,1,16]{5,4,3,2,0,1:T(1,128)} copy(f32[3,128,7,7,1,16]{1,5,3,2,0,4:T(8,128)S(1)} %convolution_bitcast_fusion.1) | data formatting | bytes 2408448 | tf_op jit(solution)/shard_map/cp,fp...->fc.../transpose | solution.py:82
  118.0 33.9 %reduce.1 = f32[128,3,7,7,16]{4,3,2,1,0:T(8,128)} reduce(f32[128,3,7,7,1,16]{5,4,3,2,1,0:T(1,128)} %bitcast.244, f32[]{:T(128)} %broadcast.568), dimensions={4}, to_apply=%bitcast.216.reduce_sub_computation | reduce | bytes 2408452
  151.9 9.2 %reshape.476 = f32[8,1,37632]{2,1,0:T(1,128)} reshape(f32[128,3,7,7,16]{4,3,2,1,0:T(8,128)} %reduce.1) | data formatting | bytes 2408448
  164.8 9.2 %copy.534 = f32[3,16,7,7,128]{4,1,0,3,2:T(8,128)S(1)} copy(f32[3,16,7,7,128]{1,3,2,0,4:T(8,128)} %bitcast.243) | data formatting | bytes 2408448 | tf_op jit(solution)/shard_map/jit(_take)/gather | solution.py:182
  174.2 8.0 %all-to-all-done.1 = f32[8,1,37632]{2,1,0:T(1,128)S(1)} async-done(((f32[8,1,37632]{2,1,0:T(1,128)}), f32[8,1,37632]{2,1,0:T(1,128)S(1)}, u32[]{:S(2)}, u32[]{:S(2)}) %all-to-all-start.1) | async-done | bytes 1204256 | tf_op jit(solution)/shard_map/all_to_all | solution.py:191
  182.2 4.9 reduce.2
  187.1 26.2 %reshape.477 = f32[128,3,7,7,1,16]{5,4,3,2,1,0:T(1,128)} reshape(f32[8,37632]{1,0:T(8,128)} %reduce.2) | data formatting | bytes 2408448
  213.3 22.7 %copy.546 = f32[3,128,7,7,1,16]{1,5,4,3,2,0:T(8,128)S(1)} copy(f32[3,128,7,7,1,16]{5,4,3,2,0,1:T(1,128)} %bitcast.245) | data formatting | bytes 2408448 | tf_op jit(solution)/shard_map/all_to_all | solution.py:191
  237.1 6.6 mul.460
  243.7 11.4 %copy.547 = f32[3,16,7,7,8,1,16]{6,4,1,0,3,2,5:T(8,128)} copy(f32[3,16,7,7,8,1,16]{1,4,6,3,2,0,5:T(8,128)} %bitcast.246) | data formatting | bytes 2408448 | tf_op jit(solution)/shard_map/mul | solution.py:195
  255.1 6.3 mul.462
  265.1 5.8 collective-permute-start.1
  282.0 7.6 %collective-permute-start.3 = (f32[1,48,7,16]{3,1,2,0:T(8,128)S(1)}, f32[1,48,7,16]{3,1,2,0:T(8,128)S(1)}, u32[]{:S(2)}, u32[]{:S(2)}) collective-permute-start(f32[1,48,7,16]{3,1,2,0:T(8,128)S(1)} %get-tuple-element.30), channel_id=1, source_target_pairs={{1,0},{2,1},{3,2},{4,3},{5,4},{6,5},{7,6},{8,7},{9,8},{10,9},{11,1... | collective-permute-start | bytes 64520 | tf_op jit(solution)/shard_map/ppermute | solution.py:25
  293.5 75.4 %all-reduce.8 = (f32[48]{0:T(128)S(1)}, f32[48]{0:T(128)S(1)}) all-reduce(f32[48]{0:T(128)S(1)} %get-tuple-element.13, f32[48]{0:T(128)S(1)} %multiply_reduce_fusion.3), channel_id=1, replica_groups=mesh['modes'=8,'mesh'=32] {'mesh'}, use_global_device_ids=true, to_apply=%region_1.2 | all-reduce | flops 96 | bytes 768 | tf_op jit(solution)/shard_map/psum | solution.py:212
  370.5 69.8 %psum.44 = f32[48]{0:T(128)S(1)} all-reduce(f32[48]{0:T(128)S(1)} %get-tuple-element.11), channel_id=1, replica_groups=mesh['modes'=8,'mesh'=32] {'mesh'}, use_global_device_ids=true, to_apply=%region_5.6 | all-reduce | flops 48 | bytes 384 | tf_op jit(solution)/shard_map/psum | solution.py:212
  446.0 3.9 collective-permute-start.4
  451.3 5.2 collective-permute-start.5
  462.3 76.0 %psum.45 = f32[48]{0:T(128)} all-reduce(f32[48]{0:T(128)} %multiply_reduce_fusion.1), channel_id=1, replica_groups=mesh['modes'=8,'mesh'=32] {'mesh'}, use_global_device_ids=true, to_apply=%region_7.8 | all-reduce | flops 48 | bytes 384 | tf_op jit(solution)/shard_map/psum | solution.py:225
  541.4 69.6 %psum.46 = f32[48]{0:T(128)S(1)} all-reduce(f32[48]{0:T(128)} %multiply_reduce_fusion), channel_id=1, replica_groups=mesh['modes'=8,'mesh'=32] {'mesh'}, use_global_device_ids=true, to_apply=%region_9.10 | all-reduce | flops 48 | bytes 384 | tf_op jit(solution)/shard_map/psum | solution.py:212
  618.9 3.9 collective-permute-start.6
  623.6 5.2 collective-permute-start.7
  633.4 75.3 %psum.47 = f32[48]{0:T(128)S(1)} all-reduce(f32[48]{0:T(128)S(1)} %fusion.37), channel_id=1, replica_groups=mesh['modes'=8,'mesh'=32] {'mesh'}, use_global_device_ids=true, to_apply=%region_11.12 | all-reduce | flops 48 | bytes 384 | tf_op jit(solution)/shard_map/psum | solution.py:225
  (182 shorter events, 71.8 us)
Async XLA Ops:
  38.3 22.1 %all-to-all-start = ((f32[8,1,37632]{2,1,0:T(1,128)}), f32[8,1,37632]{2,1,0:T(1,128)S(1)}, u32[]{:S(2)}, u32[]{:S(2)}) async-start(f32[8,1,37632]{2,1,0:T(1,128)} %reshape.474), calls=%async_computation | async-start | bytes 2408448 | tf_op jit(solution)/shard_map/all_to_all | solution.py:185
  84.2 6.3 copy-start.12
  90.5 1.1 copy-start.11
  95.3 2.9 copy-start.10
  161.1 21.1 %all-to-all-start.1 = ((f32[8,1,37632]{2,1,0:T(1,128)}), f32[8,1,37632]{2,1,0:T(1,128)S(1)}, u32[]{:S(2)}, u32[]{:S(2)}) async-start(f32[8,1,37632]{2,1,0:T(1,128)} %reshape.476), calls=%async_computation.1 | async-start | bytes 2408448 | tf_op jit(solution)/shard_map/all_to_all | solution.py:191
  164.8 9.3 %copy-start.13 = (f32[7]{0:T(128)S(1)}, f32[7]{0:T(128)}, u32[]{:S(2)}) copy-start(f32[7]{0:T(128)} %constant.116.clone) | copy-start | bytes 88
  164.8 9.3 %copy-start.28 = (f32[7]{0:T(128)S(1)}, f32[7]{0:T(128)}, u32[]{:S(2)}) copy-start(f32[7]{0:T(128)} %constant.138) | copy-start | bytes 88
  174.0 119.0 %copy-start.21 = (pred[128]{0:T(512)(128)(4,1)}, pred[128]{0:T(512)(128)(4,1)S(1)}, u32[]{:S(2)}) copy-start(pred[128]{0:T(512)(128)(4,1)S(1)} %broadcast_compare_fusion.7) | copy-start | bytes 388
  174.1 118.7 %copy-start.16 = (pred[128]{0:T(512)(128)(4,1)}, pred[128]{0:T(512)(128)(4,1)S(1)}, u32[]{:S(2)}) copy-start(pred[128]{0:T(512)(128)(4,1)S(1)} %broadcast_compare_fusion.3) | copy-start | bytes 388
  261.7 11.1 %collective-permute-start = (f32[1,48,7,16]{3,1,2,0:T(8,128)S(1)}, f32[1,48,7,16]{3,1,2,0:T(8,128)S(1)}, u32[]{:S(2)}, u32[]{:S(2)}) collective-permute-start(f32[1,48,7,16]{3,1,2,0:T(8,128)S(1)} %get-tuple-element.33), channel_id=1, source_target_pairs={{0,1},{1,2},{2,3},{3,4},{4,5},{5,6},{6,7},{7,8},{8,9},{9,10},{10,1... | collective-permute-start | bytes 64520 | tf_op jit(solution)/shard_map/ppermute | solution.py:24
  265.1 8.9 %collective-permute-start.1 = (f32[1,48,7,16]{3,1,2,0:T(8,128)S(1)}, f32[1,48,7,16]{3,1,2,0:T(8,128)S(1)}, u32[]{:S(2)}, u32[]{:S(2)}) collective-permute-start(f32[1,48,7,16]{3,1,2,0:T(8,128)S(1)} %get-tuple-element.34), channel_id=1, source_target_pairs={{1,0},{2,1},{3,2},{4,3},{5,4},{6,5},{7,6},{8,7},{9,8},{10,9},{11,1... | collective-permute-start | bytes 64520 | tf_op jit(solution)/shard_map/ppermute | solution.py:25
  274.4 1.1 copy-start.6
  280.0 11.1 %collective-permute-start.2 = (f32[1,48,7,16]{3,1,2,0:T(8,128)S(1)}, f32[1,48,7,16]{3,1,2,0:T(8,128)S(1)}, u32[]{:S(2)}, u32[]{:S(2)}) collective-permute-start(f32[1,48,7,16]{3,1,2,0:T(8,128)S(1)} %get-tuple-element.29), channel_id=1, source_target_pairs={{0,1},{1,2},{2,3},{3,4},{4,5},{5,6},{6,7},{7,8},{8,9},{9,10},{10,1... | collective-permute-start | bytes 64520 | tf_op jit(solution)/shard_map/ppermute | solution.py:24
  282.0 10.5 %collective-permute-start.3 = (f32[1,48,7,16]{3,1,2,0:T(8,128)S(1)}, f32[1,48,7,16]{3,1,2,0:T(8,128)S(1)}, u32[]{:S(2)}, u32[]{:S(2)}) collective-permute-start(f32[1,48,7,16]{3,1,2,0:T(8,128)S(1)} %get-tuple-element.30), channel_id=1, source_target_pairs={{1,0},{2,1},{3,2},{4,3},{5,4},{6,5},{7,6},{8,7},{9,8},{10,9},{11,1... | collective-permute-start | bytes 64520 | tf_op jit(solution)/shard_map/ppermute | solution.py:25
  292.8 76.2 %copy-start.1 = (f32[48,7,5,128]{3,0,1,2:T(8,128)}, f32[48,7,5,128]{3,0,1,2:T(8,128)S(1)}, u32[]{:S(2)}) copy-start(f32[48,7,5,128]{3,0,1,2:T(8,128)S(1)} %pad_maximum_fusion.5) | copy-start | bytes 2580484
  292.9 76.1 %copy-start.4 = (f32[48,7,128]{2,0,1:T(8,128)}, f32[48,7,128]{2,0,1:T(8,128)S(1)}, u32[]{:S(2)}) copy-start(f32[48,7,128]{2,0,1:T(8,128)S(1)} %get-tuple-element.15) | copy-start | bytes 516100
  293.1 75.9 %copy-start.5 = (f32[48,7,128]{2,0,1:T(8,128)}, f32[48,7,128]{2,0,1:T(8,128)S(1)}, u32[]{:S(2)}) copy-start(f32[48,7,128]{2,0,1:T(8,128)S(1)} %select_add_fusion.2) | copy-start | bytes 516100
  440.3 1.5 copy-start.31
  446.0 10.6 %collective-permute-start.4 = (f32[1,48,7,16]{3,1,2,0:T(8,128)S(1)}, f32[1,48,7,16]{3,1,2,0:T(8,128)S(1)}, u32[]{:S(2)}, u32[]{:S(2)}) collective-permute-start(f32[1,48,7,16]{3,1,2,0:T(8,128)S(1)} %get-tuple-element.25), channel_id=1, source_target_pairs={{0,1},{1,2},{2,3},{3,4},{4,5},{5,6},{6,7},{7,8},{8,9},{9,10},{10,1... | collective-permute-start | bytes 64520 | tf_op jit(solution)/shard_map/ppermute | solution.py:24
  451.3 8.2 %collective-permute-start.5 = (f32[1,48,7,16]{3,1,2,0:T(8,128)S(1)}, f32[1,48,7,16]{3,1,2,0:T(8,128)S(1)}, u32[]{:S(2)}, u32[]{:S(2)}) collective-permute-start(f32[1,48,7,16]{3,1,2,0:T(8,128)S(1)} %get-tuple-element.26), channel_id=1, source_target_pairs={{1,0},{2,1},{3,2},{4,3},{5,4},{6,5},{7,6},{8,7},{9,8},{10,9},{11,1... | collective-permute-start | bytes 64520 | tf_op jit(solution)/shard_map/ppermute | solution.py:25
  461.2 78.2 %copy-start = (f32[48,7,7,128]{3,0,1,2:T(8,128)S(1)}, f32[48,7,7,128]{3,0,1,2:T(8,128)}, u32[]{:S(2)}) copy-start(f32[48,7,7,128]{3,0,1,2:T(8,128)} %get-tuple-element.12) | copy-start | bytes 3612676
  612.2 1.8 copy-start.26
  612.2 1.8 copy-start.9
  615.7 1.7 copy-start.14
  618.0 5.4 copy-start.25
  618.1 5.5 copy-start.27
  618.9 11.0 %collective-permute-start.6 = (f32[1,48,7,16]{3,1,2,0:T(8,128)}, f32[1,48,7,16]{3,1,2,0:T(8,128)}, u32[]{:S(2)}, u32[]{:S(2)}) collective-permute-start(f32[1,48,7,16]{3,1,2,0:T(8,128)} %get-tuple-element.21), channel_id=1, source_target_pairs={{0,1},{1,2},{2,3},{3,4},{4,5},{5,6},{6,7},{7,8},{8,9},{9,10},{10,1... | collective-permute-start | bytes 64520 | tf_op jit(solution)/shard_map/ppermute | solution.py:24
  623.6 8.5 %collective-permute-start.7 = (f32[1,48,7,16]{3,1,2,0:T(8,128)}, f32[1,48,7,16]{3,1,2,0:T(8,128)S(1)}, u32[]{:S(2)}, u32[]{:S(2)}) collective-permute-start(f32[1,48,7,16]{3,1,2,0:T(8,128)} %get-tuple-element.22), channel_id=1, source_target_pairs={{1,0},{2,1},{3,2},{4,3},{5,4},{6,5},{7,6},{8,7},{9,8},{10,9},{11,1... | collective-permute-start | bytes 64520 | tf_op jit(solution)/shard_map/ppermute | solution.py:25
  631.0 1.3 copy-start.18
  632.9 75.8 %copy-start.30 = (f32[48]{0:T(128)S(1)}, f32[48]{0:T(128)}, u32[]{:S(2)}) copy-start(f32[48]{0:T(128)} %copy-done.29) | copy-start | bytes 580
  632.9 75.9 %copy-start.19 = (f32[3,16]{1,0:T(4,128)S(1)}, f32[3,16]{1,0:T(4,128)}, u32[]{:S(2)}) copy-start(f32[3,16]{1,0:T(4,128)} %mul.487) | copy-start | bytes 580
  633.0 75.9 %copy-start.20 = (f32[3,16]{1,0:T(4,128)S(1)}, f32[3,16]{1,0:T(4,128)}, u32[]{:S(2)}) copy-start(f32[3,16]{1,0:T(4,128)} %mul.510) | copy-start | bytes 580
  (10 other events, 7.1 us)
where the time goes:
time: 719 us; the launch traced here: 712 us
  blocking collectives  366 us (51%)
  local copies, waits for them, and re-layouts  172 us (24%)
  other arithmetic  73.8 us (10%)
  starting transfers between devices  45.6 us (6%)
  waiting for transfers between devices  35.2 us (5%)
  matrix products  18.2 us (3%)
    psum x3, blocking collectives, squares(): return lax.psum(weighted_inner(values, values), 'mesh')  215 us
    psum x2, blocking collectives, shards(): step_size = norm_now / lax.psum(weighted_inner(direction, applied), 'mesh')  151 us
    unnamed x70, local copies, waits for them, and re-layouts  62.5 us
    unnamed x2, other arithmetic  44.1 us
    mul x3, local copies, waits for them, and re-layouts, shards(): STEP_TIME * nonlinear_modes  24.2 us
    ppermute x4, starting transfers between devices, with_halo(): after = lax.ppermute(leading, axis, down)  23.9 us
    all_to_all x1, local copies, waits for them, and re-layouts, shards(): lax.all_to_all(result, 'modes', split_axis=1, concat_axis=4, tiled=True)  22.7 us
    gather x2, local copies, waits for them, and re-layouts, shards(): grid_field = jnp.take(velocity, element_slot, axis=4)  19.5 us
  transfers between devices with their start and end apart: 10, of which 9 were waited for; matrix products, arithmetic and copies ran while one was open for 2% of the time, Pallas kernels for 0%

commit v1 on v0

v1 whole, which is shorter than its diff:
```python
import functools

import jax
import jax.numpy as jnp
import numpy as np
from jax import lax
from jax.experimental import pallas as pl
from jax.experimental.pallas import tpu as pltpu
from jax.sharding import PartitionSpec as P

NODES = 7
FIELDS = 3
GROUPS = 8
LOCAL = 16
NCOEF = 128
LANES = 128
EY = 16
PLANES_PER_FIELD = NODES * NODES
SIGMA_BASE = 8.0
SPAN_WAVE = 0.25
STEP_TIME = 0.01
MOMENTS = 6


def gll_tables():
    inner_point = np.sqrt((5.0 - 2.0 * np.sqrt(5.0 / 3.0)) / 11.0)
    outer_point = np.sqrt((5.0 + 2.0 * np.sqrt(5.0 / 3.0)) / 11.0)
    points = np.array([-1.0, -outer_point, -inner_point, 0.0, inner_point, outer_point, 1.0])
    legendre_prev = points * 0.0 + 1.0
    legendre_now = points.copy()
    for degree in range(1, points.shape[0] - 1):
        legendre_next = ((2 * degree + 1) * points * legendre_now - degree * legendre_prev) / (
            degree + 1
        )
        legendre_prev = legendre_now
        legendre_now = legendre_next
    order_value = points.shape[0] - 1
    quadrature = 2.0 / (order_value * (order_value + 1) * legendre_now**2)
    counter = np.arange(points.shape[0])
    same_node = counter[:, None] == counter[None, :]
    distances = np.where(same_node, 1.0, points[:, None] - points[None, :])
    barycentric = 1.0 / np.prod(distances, axis=1)
    off_diagonal = np.where(same_node, 0.0, barycentric[None, :] / barycentric[:, None] / distances)
    derivative = np.where(same_node, -np.sum(off_diagonal, axis=1)[:, None], off_diagonal)
    stiffness = derivative.T @ (quadrature[:, None] * derivative)
    return quadrature, derivative, stiffness


def fourier_tables():
    half_count = NCOEF // 2
    planes = np.arange(NCOEF) * 2.0 * np.pi / NCOEF
    numbers = np.arange(NCOEF)
    wavenumber = np.where(numbers <= half_count, numbers, numbers - half_count)
    cosine_mask = (numbers <= half_count)[None, :]
    phase = planes[:, None] * wavenumber[None, :]
    inverse = np.where(cosine_mask, np.cos(phase), np.sin(phase))
    slope = SPAN_WAVE * wavenumber[None, :] * np.where(cosine_mask, -np.sin(phase), np.cos(phase))
    normaliser = np.where((numbers == 0) | (numbers == half_count), 1.0 / NCOEF, 2.0 / NCOEF)
    forward = normaliser[:, None] * inverse.T
    return inverse, slope, forward


QUAD, DERIV, STIFF = gll_tables()
SCALED_STIFF = STIFF / QUAD[:, None]
MASS = 0.25 * QUAD[:, None] * QUAD[None, :]


def split_table(table):
    high = np.asarray(table, np.float32).astype(jnp.bfloat16)
    low = (np.asarray(table, np.float64) - high.astype(np.float64)).astype(jnp.bfloat16)
    return high, low


def transform_tables():
    inverse, slope, forward = fourier_tables()
    t_high, t_low = split_table(np.concatenate([inverse, slope], axis=0))
    f_high, f_low = split_table(-STEP_TIME * forward)
    padded = np.zeros((8, 8))
    padded[:NODES, :NODES] = 2.0 * DERIV
    b_high, b_low = split_table(np.kron(padded.T, np.eye(EY)))
    return [
        np.concatenate([t_high, t_high], axis=1),
        t_low,
        np.concatenate([f_high, f_high], axis=1),
        f_low,
        np.concatenate([b_high, b_high], axis=0),
        b_low,
    ]


def split_value(value):
    high = value.astype(jnp.bfloat16)
    low = (value - high.astype(jnp.float32)).astype(jnp.bfloat16)
    return high, low


def dot(left, right):
    return jnp.dot(left, right, preferred_element_type=jnp.float32)


def swap_groups(tiles, group):
    tiles = list(tiles)
    for bit in (4, 2, 1):
        low = (group & bit) == 0
        new = list(tiles)
        for at in range(8):
            if at & bit:
                continue
            first, second = tiles[at], tiles[at + bit]
            if bit == 4:
                moved = pltpu.roll(jnp.where(low, second, first), 64, 1)
                new[at] = jnp.where(low, first, moved)
                new[at + bit] = jnp.where(low, moved, second)
            else:
                new[at] = jnp.where(low, first, pltpu.roll(second, EY * bit, 1))
                new[at + bit] = jnp.where(low, pltpu.roll(first, LANES - EY * bit, 1), second)
        tiles = new
    return tiles


def weighted_sum(coefficients, values):
    total = None
    for coefficient, value in zip(coefficients, values):
        term = float(coefficient) * value
        total = term if total is None else total + term
    return total


def line_product(matrix, line, sign):
    even = [line[k] + line[6 - k] for k in range(3)] + [line[3]]
    odd = [line[k] - line[6 - k] for k in range(3)]
    out = [None] * 7
    for i in range(3):
        even_row = [0.5 * (matrix[i, k] + matrix[i, 6 - k]) for k in range(3)] + [matrix[i, 3]]
        odd_row = [0.5 * (matrix[i, k] - matrix[i, 6 - k]) for k in range(3)]
        even_part = weighted_sum(even_row, even)
        odd_part = weighted_sum(odd_row, odd)
        out[i] = even_part + odd_part
        out[6 - i] = even_part - odd_part if sign > 0 else odd_part - even_part
    if sign > 0:
        out[3] = weighted_sum([matrix[3, k] for k in range(4)], even)
    else:
        out[3] = weighted_sum([matrix[3, k] for k in range(3)], odd)
    return out


def kernel(
    mesh_x,
    mesh_z,
    vel,
    slot,
    tt,
    tl,
    ff,
    fl,
    bb,
    bl,
    out,
    msg,
    recv1,
    phys,
    span,
    cross,
    send2,
    recv2,
    basis,
    moments,
    halo_send,
    halo_recv,
    red_x,
    red_z,
    send1_sem,
    recv1_sem,
    own1_sem,
    send2_sem,
    recv2_sem,
    own2_sem,
    halo_send_sem,
    halo_recv_sem,
    redx_send_sem,
    redx_recv_sem,
    redz_send_sem,
    redz_recv_sem,
):
    me = lax.axis_index("modes")
    strip = lax.axis_index("mesh")
    strips = mesh_x * mesh_z
    at_x = lax.rem(strip, mesh_x)
    at_z = strip // mesh_x
    following = lax.rem(strip + 1, strips)
    previous = lax.rem(strip + strips - 1, strips)

    def mode_peer(step):
        return lax.rem(me + step, GROUPS)

    def x_peer(step):
        return at_z * mesh_x + lax.rem(at_x + step, mesh_x)

    def z_peer(step):
        return lax.rem(at_z + step, mesh_z) * mesh_x + at_x

    barrier = pltpu.get_barrier_semaphore()
    greeted = [{"modes": mode_peer(step)} for step in range(1, GROUPS)]
    greeted += [{"mesh": following}, {"mesh": previous}]
    greeted += [{"mesh": x_peer(step)} for step in range(1, mesh_x)]
    greeted += [{"mesh": z_peer(step)} for step in range(1, mesh_z)]
    for device in greeted:
        pl.semaphore_signal(
            barrier, inc=1, device_id=device, device_id_type=pl.DeviceIdType.MESH
        )

    lane = lax.broadcasted_iota(jnp.int32, (8, LANES), 1)
    group = lane // EY
    row = lane % EY
    slots = jnp.broadcast_to(slot[...], (8, LANES))

    def remote(src, dst, send, recv, device):
        return pltpu.make_async_remote_copy(
            src_ref=src,
            dst_ref=dst,
            send_sem=send,
            recv_sem=recv,
            device_id=device,
            device_id_type=pl.DeviceIdType.MESH,
        )

    def out_copy(f, step):
        peer = mode_peer(step)
        return remote(
            msg.at[peer, pl.ds(f * NODES, NODES)],
            recv1.at[pl.ds(f * NODES, NODES), pl.ds(me * LOCAL, LOCAL)],
            send1_sem.at[f, step - 1],
            recv1_sem.at[f, step - 1],
            {"modes": peer},
        )

    def own_out(f):
        return pltpu.make_async_copy(
            msg.at[me, pl.ds(f * NODES, NODES)],
            recv1.at[pl.ds(f * NODES, NODES), pl.ds(me * LOCAL, LOCAL)],
            own1_sem.at[f],
        )

    def back_copy(f, step):
        peer = mode_peer(step)
        return remote(
            send2.at[pl.ds(f * NODES, NODES), pl.ds(peer * LOCAL, LOCAL)],
            recv2.at[me, pl.ds(f * NODES, NODES)],
            send2_sem.at[f, step - 1],
            recv2_sem.at[f, step - 1],
            {"modes": peer},
        )

    def own_back(f):
        return pltpu.make_async_copy(
            send2.at[pl.ds(f * NODES, NODES), pl.ds(me * LOCAL, LOCAL)],
            recv2.at[me, pl.ds(f * NODES, NODES)],
            own2_sem.at[f],
        )

    def spread_rows(f, i):
        for half in range(2):
            rows = pl.ds(8 * half, 8)
            tiles = []
            for j in range(NODES):
                at = f * PLANES_PER_FIELD + i * NODES + j
                tile = jnp.take_along_axis(vel[at, rows, :], slots, axis=1)
                out[at, rows, :] = SIGMA_BASE * tile
                tiles.append(tile)
            tiles = swap_groups(tiles + [jnp.zeros((8, LANES), jnp.float32)], group)
            for k in range(GROUPS):
                msg[k, f * NODES + i, rows, :] = tiles[k]

    for f in range(FIELDS):
        lax.fori_loop(0, NODES, lambda i, c, f=f: (spread_rows(f, i), c)[1], 0)
        if f == 0:
            pl.semaphore_wait(barrier, len(greeted))
        for step in range(1, GROUPS):
            out_copy(f, step).start()
        own_out(f).start()

    def to_planes(f, carry):
        for step in range(1, GROUPS):
            out_copy(f, step).wait_recv()
        own_out(f).wait()
        for i in range(NODES):
            at = f * NODES + i
            high, low = split_value(recv1[at])
            value = dot(tt[...], jnp.concatenate([high, low], axis=0)) + dot(tl[...], high)
            planes = value[:NCOEF]
            phys[at] = planes
            span[at] = value[NCOEF:]
            high, low = split_value(planes)
            cross[at] = dot(jnp.concatenate([high, low], axis=1), bb[...]) + dot(high, bl[...])
        return carry

    lax.fori_loop(0, FIELDS, to_planes, 0)

    def advect(f, carry):
        def rows_of(block, inner):
            rows = pl.ds(pl.multiple_of(block * 8, 8), 8)
            line = [phys[f * NODES + i, rows, :] for i in range(NODES)]
            stream = line_product(2.0 * DERIV, line, -1)
            for i in range(NODES):
                at = f * NODES + i
                send2[at, rows, :] = (
                    phys[i, rows, :] * stream[i]
                    + phys[NODES + i, rows, :] * cross[at, rows, :]
                    + phys[2 * NODES + i, rows, :] * span[at, rows, :]
                )
            return inner

        lax.fori_loop(0, NCOEF // 8, rows_of, 0)
        for i in range(NODES):
            at = f * NODES + i
            high, low = split_value(send2[at])
            send2[at] = dot(ff[...], jnp.concatenate([high, low], axis=0)) + dot(fl[...], high)
        for step in range(1, GROUPS):
            back_copy(f, step).start()
        own_back(f).start()
        return carry

    lax.fori_loop(0, FIELDS, advect, 0)

    def gather_source(f, carry):
        for step in range(1, GROUPS):
            back_copy(f, step).wait_recv()
        own_back(f).wait()
        for half in range(2):
            rows = pl.ds(8 * half, 8)
            for i in range(NODES):
                tiles = swap_groups(
                    [recv2[k, f * NODES + i, rows, :] for k in range(GROUPS)], group
                )
                for j in range(NODES):
                    at = f * PLANES_PER_FIELD + i * NODES + j
                    basis[0, at, rows, :] = float(MASS[i, j]) * (out[at, rows, :] + tiles[j])
        return carry

    lax.fori_loop(0, FIELDS, gather_source, 0)

    is_first = strip == 0
    is_last = strip == strips - 1
    inflow = jnp.logical_and(group == 0, is_first)
    not_inflow = jnp.logical_not(inflow)
    west = group == 0
    east = group == GROUPS - 1
    south = row != 0
    north = row != EY - 1
    has_previous = jnp.where(is_first, 0.0, 1.0)
    has_following = jnp.where(is_last, 0.0, 1.0)
    east_weight = jnp.where(jnp.logical_and(east, is_last), 1.0, 0.5)

    def halo_copies(level):
        return (
            remote(
                halo_send.at[level, 0],
                halo_recv.at[level, 0],
                halo_send_sem.at[level, 0],
                halo_recv_sem.at[level, 0],
                {"mesh": following},
            ),
            remote(
                halo_send.at[level, 1],
                halo_recv.at[level, 1],
                halo_send_sem.at[level, 1],
                halo_recv_sem.at[level, 1],
                {"mesh": previous},
            ),
        )

    def at_block(block):
        f = block // 2
        rows = pl.ds(pl.multiple_of((block % 2) * 8, 8), 8)
        return f, rows

    def send_faces(level):
        def pack(block, carry):
            f, rows = at_block(block)
            base = f * PLANES_PER_FIELD
            to_next = jnp.zeros((8, LANES), jnp.float32)
            to_prior = to_next
            for j in range(NODES):
                right = basis[level, base + 6 * NODES + j, rows, :]
                left = basis[level, base + j, rows, :]
                here = group == j
                to_next = jnp.where(here, pltpu.roll(right, (EY * (j + 1)) % LANES, 1), to_next)
                to_prior = jnp.where(
                    here, pltpu.roll(left, EY * j, 1) if j else left, to_prior
                )
            halo_send[level, 0, f, rows, :] = to_next
            halo_send[level, 1, f, rows, :] = to_prior
            return carry

        lax.fori_loop(0, 2 * FIELDS, pack, 0)
        for copy in halo_copies(level):
            copy.start()

    def along_rows(line):
        bottom, top = line[0], line[6]
        line[0] = jnp.where(south, bottom + pltpu.roll(top, 1, 1), 0.0)
        line[6] = jnp.where(north, top + pltpu.roll(bottom, LANES - 1, 1), 0.0)
        return line

    def squares(line, edge):
        total = line[1] * line[1]
        for j in range(2, 6):
            total = total + line[j] * line[j]
        return total + 0.5 * (line[0] * line[0] + line[6] * line[6])

    def finish_inside(level):
        def block_of(block, carry):
            f, rows = at_block(block)
            base = f * PLANES_PER_FIELD
            total = jnp.zeros((8, LANES), jnp.float32)
            for i in range(1, 6):
                line = [basis[level, base + i * NODES + j, rows, :] for j in range(NODES)]
                line = along_rows(line)
                basis[level, base + i * NODES, rows, :] = line[0]
                basis[level, base + i * NODES + 6, rows, :] = line[6]
                total = total + squares(line, None)
            moments[2 * level, f, rows, :] = total
            return carry

        lax.fori_loop(0, 2 * FIELDS, block_of, 0)

    def finish_faces(level):
        for copy in halo_copies(level):
            copy.wait_recv()

        def block_of(block, carry):
            f, rows = at_block(block)
            base = f * PLANES_PER_FIELD
            prior = halo_recv[level, 0, f, rows, :] * has_previous
            after = halo_recv[level, 1, f, rows, :] * has_following
            lefts, rights = [], []
            for j in range(NODES):
                left = basis[level, base + j, rows, :]
                right = basis[level, base + 6 * NODES + j, rows, :]
                from_prior = pltpu.roll(prior, LANES - EY * j, 1) if j else prior
                from_after = pltpu.roll(after, LANES - EY * (j + 1), 1) if j < 7 else after
                lefts.append(left + jnp.where(west, from_prior, pltpu.roll(right, EY, 1)))
                rights.append(
                    right + jnp.where(east, from_after, pltpu.roll(left, LANES - EY, 1))
                )
            lefts = [jnp.where(not_inflow, value, 0.0) for value in along_rows(lefts)]
            rights = along_rows(rights)
            for j in range(NODES):
                basis[level, base + j, rows, :] = lefts[j]
                basis[level, base + 6 * NODES + j, rows, :] = rights[j]
            moments[2 * level, f, rows, :] = (
                moments[2 * level, f, rows, :]
                + 0.5 * squares(lefts, None)
                + east_weight * squares(rights, None)
            )
            return carry

        lax.fori_loop(0, 2 * FIELDS, block_of, 0)

    def operate(level, keep_image):
        def block_of(block, carry):
            f, rows = at_block(block)
            base = f * PLANES_PER_FIELD
            number = (
                me * LOCAL
                + (block % 2) * 8
                + lax.broadcasted_iota(jnp.int32, (8, LANES), 0)
            )
            wave = SPAN_WAVE * jnp.where(number <= NCOEF // 2, number, number - NCOEF // 2).astype(
                jnp.float32
            )
            shift = 0.25 * (SIGMA_BASE + wave * wave)
            values = [basis[level, base + n, rows, :] for n in range(PLANES_PER_FIELD)]
            image = [None] * PLANES_PER_FIELD
            for j in range(NODES):
                line = line_product(SCALED_STIFF, [values[i * NODES + j] for i in range(NODES)], 1)
                for i in range(NODES):
                    image[i * NODES + j] = line[i]
            energy = jnp.zeros((8, LANES), jnp.float32)
            for i in range(NODES):
                line = line_product(SCALED_STIFF, values[i * NODES : (i + 1) * NODES], 1)
                for j in range(NODES):
                    n = i * NODES + j
                    result = float(QUAD[i] * QUAD[j]) * (image[n] + line[j] + shift * values[n])
                    energy = energy + result * values[n]
                    if keep_image:
                        basis[level + 1, base + n, rows, :] = result
            moments[2 * level + 1, f, rows, :] = energy
            return carry

        lax.fori_loop(0, 2 * FIELDS, block_of, 0)

    for level in range(3):
        send_faces(level)
        finish_inside(level)
        finish_faces(level)
        operate(level, level < 2)

    packed = jnp.zeros((8, LANES), jnp.float32)
    for m in range(MOMENTS):
        for block in range(2 * FIELDS):
            f, half = block // 2, block % 2
            total = jnp.sum(moments[m, f, 8 * half : 8 * half + 8, :], axis=1, keepdims=True)
            packed = jnp.where(lane == 8 * block + m, total, packed)

    def sum_over(value, slots_ref, mine, count, copies):
        slots_ref[mine] = value
        for copy in copies:
            copy.start()
        for copy in copies:
            copy.wait_recv()
        total = slots_ref[0]
        for k in range(1, count):
            total = total + slots_ref[k]
        return total

    x_copies = [
        remote(
            red_x.at[at_x],
            red_x.at[at_x],
            redx_send_sem.at[step - 1],
            redx_recv_sem.at[step - 1],
            {"mesh": x_peer(step)},
        )
        for step in range(1, mesh_x)
    ]
    z_copies = [
        remote(
            red_z.at[at_z],
            red_z.at[at_z],
            redz_send_sem.at[step - 1],
            redz_recv_sem.at[step - 1],
            {"mesh": z_peer(step)},
        )
        for step in range(1, mesh_z)
    ]
    packed = sum_over(packed, red_x, at_x, mesh_x, x_copies)
    packed = sum_over(packed, red_z, at_z, mesh_z, z_copies)

    m0, m1, m2, m3, m4, m5 = [
        packed if m == 0 else pltpu.roll(packed, LANES - m, 1) for m in range(MOMENTS)
    ]
    s0, s1, s2 = lax.rsqrt(m1), lax.rsqrt(m3), lax.rsqrt(m5)
    l10 = m2 * s0 * s1
    l20 = m3 * s0 * s2
    h21 = m4 * s1 * s2
    d1 = 1.0 - l10 * l10
    l21 = (h21 - l20 * l10) / d1
    d2 = 1.0 - l20 * l20 - l21 * l21 * d1
    y0 = m0 * s0
    y1 = m1 * s1 - l10 * y0
    y2 = m2 * s2 - l20 * y0 - l21 * y1
    c2 = y2 / d2
    c1 = y1 / d1 - l21 * c2
    c0 = y0 - l10 * c1 - l20 * c2
    c0, c1, c2 = c0 * s0, c1 * s1, c2 * s2

    for block in range(2 * FIELDS):
        f, half = block // 2, block % 2
        rows = pl.ds(8 * half, 8)
        f0, f1, f2 = [
            jnp.broadcast_to(c[:, 8 * block : 8 * block + 1], (8, LANES)) for c in (c0, c1, c2)
        ]

        def combine(n, carry, f=f, rows=rows, f0=f0, f1=f1, f2=f2):
            at = f * PLANES_PER_FIELD + n
            out[at, rows, :] = (
                f0 * basis[0, at, rows, :] + f1 * basis[1, at, rows, :] + f2 * basis[2, at, rows, :]
            )
            return carry

        lax.fori_loop(0, PLANES_PER_FIELD, combine, 0, unroll=7)

    for f in range(FIELDS):
        for step in range(1, GROUPS):
            out_copy(f, step).wait_send()
            back_copy(f, step).wait_send()
    for level in range(3):
        for copy in halo_copies(level):
            copy.wait_send()
    for copy in x_copies + z_copies:
        copy.wait_send()


def shards(mesh_x, mesh_z, velocity, element_slot):
    tables = [jnp.asarray(table) for table in transform_tables()]
    count = FIELDS * PLANES_PER_FIELD
    field = jnp.transpose(velocity, (0, 2, 3, 1, 4)).reshape(count, LOCAL, LANES)
    vmem = pl.BlockSpec(memory_space=pltpu.VMEM)
    lines = FIELDS * NODES
    f32 = jnp.float32
    dma = pltpu.SemaphoreType.DMA
    result = pl.pallas_call(
        functools.partial(kernel, mesh_x, mesh_z),
        out_shape=jax.ShapeDtypeStruct((count, LOCAL, LANES), f32),
        in_specs=[vmem] * 8,
        out_specs=vmem,
        scratch_shapes=[
            pltpu.VMEM((GROUPS, lines, LOCAL, LANES), f32),
            pltpu.VMEM((lines, NCOEF, LANES), f32),
            pltpu.VMEM((lines, NCOEF, LANES), f32),
            pltpu.VMEM((lines, NCOEF, LANES), f32),
            pltpu.VMEM((lines, NCOEF, LANES), f32),
            pltpu.VMEM((lines, NCOEF, LANES), f32),
            pltpu.VMEM((GROUPS, lines, LOCAL, LANES), f32),
            pltpu.VMEM((3, count, LOCAL, LANES), f32),
            pltpu.VMEM((MOMENTS, FIELDS, LOCAL, LANES), f32),
            pltpu.VMEM((3, 2, FIELDS, LOCAL, LANES), f32),
            pltpu.VMEM((3, 2, FIELDS, LOCAL, LANES), f32),
            pltpu.VMEM((mesh_x, 8, LANES), f32),
            pltpu.VMEM((mesh_z, 8, LANES), f32),
            dma((FIELDS, GROUPS - 1)),
            dma((FIELDS, GROUPS - 1)),
            dma((FIELDS,)),
            dma((FIELDS, GROUPS - 1)),
            dma((FIELDS, GROUPS - 1)),
            dma((FIELDS,)),
            dma((3, 2)),
            dma((3, 2)),
            dma((mesh_x - 1,)),
            dma((mesh_x - 1,)),
            dma((mesh_z - 1,)),
            dma((mesh_z - 1,)),
        ],
        compiler_params=pltpu.CompilerParams(
            collective_id=0, has_side_effects=True, vmem_limit_bytes=40 * 1024 * 1024
        ),
    )(field, element_slot.reshape(1, LANES), *tables)
    return jnp.transpose(
        result.reshape(FIELDS, NODES, NODES, LOCAL, LANES), (0, 3, 1, 2, 4)
    )


def solution(mesh):
    strips = mesh.shape["mesh"]
    mesh_x = 4 if strips % 4 == 0 else 1
    placed = (P(None, "modes", None, None, "mesh"), P("mesh"))
    return jax.shard_map(
        functools.partial(shards, mesh_x, strips // mesh_x),
        mesh=mesh,
        in_specs=placed,
        out_specs=P(None, "modes", None, None, "mesh"),
        check_vma=False,
    )
```

time: 719 us -> 83.6 us (0.12)
  the two profiles are of different devices: /device:TPU:128 before, /device:TPU:4 now
where the time goes in v1:
time: 83.6 us; the launch traced here: 83.2 us
  Pallas kernels  75.3 us (90%)
  local copies, waits for them, and re-layouts  7.89 us (9%)
    pallas_call x1, Pallas kernels, shards(): pl.pallas_call(functools.partial(kernel, mesh_x, mesh_z), out_shape=jax.S...  75.3 us
    unnamed x17, local copies, waits for them, and re-layouts  7.89 us

profile of v1, /device:TPU:4, one launch (start us, length us, event | category | flops | bytes accessed | tf_op | source)
XLA Modules:
  0.0 83.2 jit_solution(9136868122382485583)
XLA Ops:
  0.0 0.0 copy-start
  0.0 1.3 %copy-done = f32[3,16,7,7,128]{4,1,3,2,0:T(8,128)S(1)} copy-done((f32[3,16,7,7,128]{4,1,3,2,0:T(8,128)S(1)}, f32[3,16,7,7,128]{4,1,3,2,0:T(8,128)}, u32[]{:S(2)}) %copy-start) | copy-done | bytes 1204248
  1.3 0.0 copy-start.1
  1.3 0.9 %copy-done.1 = bf16[256,256]{1,0:T(8,128)(2,1)S(1)} copy-done((bf16[256,256]{1,0:T(8,128)(2,1)S(1)}, bf16[256,256]{1,0:T(8,128)(2,1)}, u32[]{:S(2)}) %copy-start.1) | copy-done | bytes 131096
  2.2 0.0 copy-start.2
  2.2 0.8 %copy-done.2 = bf16[256,128]{1,0:T(8,128)(2,1)S(1)} copy-done((bf16[256,128]{1,0:T(8,128)(2,1)S(1)}, bf16[256,128]{1,0:T(8,128)(2,1)}, u32[]{:S(2)}) %copy-start.2) | copy-done | bytes 65560
  3.0 0.0 copy-start.3
  3.0 0.8 %copy-done.3 = bf16[128,256]{1,0:T(8,128)(2,1)S(1)} copy-done((bf16[128,256]{1,0:T(8,128)(2,1)S(1)}, bf16[128,256]{1,0:T(8,128)(2,1)}, u32[]{:S(2)}) %copy-start.3) | copy-done | bytes 65560
  3.9 0.0 copy-start.4
  3.9 0.8 %copy-done.4 = bf16[256,128]{1,0:T(8,128)(2,1)S(1)} copy-done((bf16[256,128]{1,0:T(8,128)(2,1)S(1)}, bf16[256,128]{1,0:T(8,128)(2,1)}, u32[]{:S(2)}) %copy-start.4) | copy-done | bytes 65560
  4.7 0.0 copy-start.5
  4.7 0.8 copy-done.5
  5.5 0.0 copy-start.6
  5.5 0.8 copy-done.6
  6.2 0.0 copy-start.7
  6.2 0.7 copy-done.7
  6.9 75.3 %shard_map.82 = f32[147,16,128]{2,1,0:T(8,128)S(1)} custom-call(f32[147,16,128]{2,1,0:T(8,128)S(1)} %bitcast.8, s32[1,128]{1,0:T(1,128)S(1)} %bitcast.9, bf16[256,256]{1,0:T(8,128)(2,1)S(1)} %copy-done.1, bf16[256,128]{1,0:T(8,128)(2,1)S(1)} %copy-done.4, bf16[128,256]{1,0:T(8,128)(2,1)S(1)} %copy-done.3, bf16[128,128]{1,0:T(8,128)(2,1)S(1)} %copy-done.6, ...), custom_call_target="tpu_custom_call" | custom-call | tf_op jit(solution)/shard_map/pallas_call | solution.py:593
  82.2 1.0 %copy.10 = f32[3,16,7,7,128]{4,1,3,2,0:T(8,128)} copy(f32[3,16,7,7,128]{4,1,3,2,0:T(8,128)S(1)} %bitcast.7) | data formatting | bytes 2408448
Async XLA Ops:
  0.0 1.3 %copy-start = (f32[3,16,7,7,128]{4,1,3,2,0:T(8,128)S(1)}, f32[3,16,7,7,128]{4,1,3,2,0:T(8,128)}, u32[]{:S(2)}) copy-start(f32[3,16,7,7,128]{4,1,3,2,0:T(8,128)} %param.8) | copy-start | bytes 3612676
  1.3 0.9 %copy-start.1 = (bf16[256,256]{1,0:T(8,128)(2,1)S(1)}, bf16[256,256]{1,0:T(8,128)(2,1)}, u32[]{:S(2)}) copy-start(bf16[256,256]{1,0:T(8,128)(2,1)} %constant.12.clone.tt) | copy-start | bytes 393220
  2.2 0.8 %copy-start.2 = (bf16[256,128]{1,0:T(8,128)(2,1)S(1)}, bf16[256,128]{1,0:T(8,128)(2,1)}, u32[]{:S(2)}) copy-start(bf16[256,128]{1,0:T(8,128)(2,1)} %constant.16.clone.bb) | copy-start | bytes 196612
  3.0 0.8 %copy-start.3 = (bf16[128,256]{1,0:T(8,128)(2,1)S(1)}, bf16[128,256]{1,0:T(8,128)(2,1)}, u32[]{:S(2)}) copy-start(bf16[128,256]{1,0:T(8,128)(2,1)} %constant.14.clone.ff) | copy-start | bytes 196612
  3.9 0.8 %copy-start.4 = (bf16[256,128]{1,0:T(8,128)(2,1)S(1)}, bf16[256,128]{1,0:T(8,128)(2,1)}, u32[]{:S(2)}) copy-start(bf16[256,128]{1,0:T(8,128)(2,1)} %constant.13.clone.tl) | copy-start | bytes 196612
  4.7 0.8 copy-start.5
  5.5 0.8 copy-start.6
  6.2 0.7 copy-start.7

commit v2 on v1

v2 whole, which is shorter than its diff:
```python
import functools

import jax
import jax.numpy as jnp
import numpy as np
from jax import lax
from jax.experimental import pallas as pl
from jax.experimental.pallas import tpu as pltpu
from jax.sharding import PartitionSpec as P

NODES = 7
FIELDS = 3
GROUPS = 8
LOCAL = 16
NCOEF = 128
LANES = 128
EY = 16
PLANES_PER_FIELD = NODES * NODES
SIGMA_BASE = 8.0
SPAN_WAVE = 0.25
STEP_TIME = 0.01
MOMENTS = 6
TILES = 19
OUT_PARTS = ((0, 7), (7, 6), (13, 6))
BACK_PARTS = ((0, 6), (6, 6), (12, 7))


def gll_tables():
    inner_point = np.sqrt((5.0 - 2.0 * np.sqrt(5.0 / 3.0)) / 11.0)
    outer_point = np.sqrt((5.0 + 2.0 * np.sqrt(5.0 / 3.0)) / 11.0)
    points = np.array([-1.0, -outer_point, -inner_point, 0.0, inner_point, outer_point, 1.0])
    legendre_prev = points * 0.0 + 1.0
    legendre_now = points.copy()
    for degree in range(1, points.shape[0] - 1):
        legendre_next = ((2 * degree + 1) * points * legendre_now - degree * legendre_prev) / (
            degree + 1
        )
        legendre_prev = legendre_now
        legendre_now = legendre_next
    order_value = points.shape[0] - 1
    quadrature = 2.0 / (order_value * (order_value + 1) * legendre_now**2)
    counter = np.arange(points.shape[0])
    same_node = counter[:, None] == counter[None, :]
    distances = np.where(same_node, 1.0, points[:, None] - points[None, :])
    barycentric = 1.0 / np.prod(distances, axis=1)
    off_diagonal = np.where(same_node, 0.0, barycentric[None, :] / barycentric[:, None] / distances)
    derivative = np.where(same_node, -np.sum(off_diagonal, axis=1)[:, None], off_diagonal)
    stiffness = derivative.T @ (quadrature[:, None] * derivative)
    return quadrature, derivative, stiffness


def fourier_tables():
    half_count = NCOEF // 2
    planes = np.arange(NCOEF) * 2.0 * np.pi / NCOEF
    numbers = np.arange(NCOEF)
    wavenumber = np.where(numbers <= half_count, numbers, numbers - half_count)
    cosine_mask = (numbers <= half_count)[None, :]
    phase = planes[:, None] * wavenumber[None, :]
    inverse = np.where(cosine_mask, np.cos(phase), np.sin(phase))
    slope = SPAN_WAVE * wavenumber[None, :] * np.where(cosine_mask, -np.sin(phase), np.cos(phase))
    normaliser = np.where((numbers == 0) | (numbers == half_count), 1.0 / NCOEF, 2.0 / NCOEF)
    forward = normaliser[:, None] * inverse.T
    return inverse, slope, forward


QUAD, DERIV, STIFF = gll_tables()
SCALED_STIFF = STIFF / QUAD[:, None]
MASS = 0.25 * QUAD[:, None] * QUAD[None, :]


def split_table(table):
    high = np.asarray(table, np.float32).astype(jnp.bfloat16)
    low = (np.asarray(table, np.float64) - high.astype(np.float64)).astype(jnp.bfloat16)
    return high, low


def transform_tables():
    inverse, slope, forward = fourier_tables()
    t_high, t_low = split_table(np.concatenate([inverse, slope], axis=0))
    f_high, f_low = split_table(-STEP_TIME * forward)
    padded = np.zeros((8, 8))
    padded[:NODES, :NODES] = 2.0 * DERIV
    b_high, b_low = split_table(np.kron(padded.T, np.eye(EY)))
    return np.concatenate(
        [
            np.concatenate([t_high, t_high], axis=1),
            np.concatenate([t_low, np.concatenate([b_high, b_high], axis=0)], axis=1),
            np.concatenate([f_high, f_high], axis=1),
            np.concatenate([f_low, b_low], axis=1),
        ],
        axis=0,
    )


def split_value(value):
    high = value.astype(jnp.bfloat16)
    low = (value - high.astype(jnp.float32)).astype(jnp.bfloat16)
    return high, low


def dot(left, right):
    return jnp.dot(left, right, preferred_element_type=jnp.float32)


def swap_groups(tiles, group):
    tiles = list(tiles)
    for bit in (4, 2, 1):
        low = (group & bit) == 0
        new = list(tiles)
        for at in range(8):
            if at & bit:
                continue
            first, second = tiles[at], tiles[at + bit]
            if bit == 4:
                moved = pltpu.roll(jnp.where(low, second, first), 64, 1)
                new[at] = jnp.where(low, first, moved)
                new[at + bit] = jnp.where(low, moved, second)
            else:
                new[at] = jnp.where(low, first, pltpu.roll(second, EY * bit, 1))
                new[at + bit] = jnp.where(low, pltpu.roll(first, LANES - EY * bit, 1), second)
        tiles = new
    return tiles


def weighted_sum(coefficients, values):
    total = None
    for coefficient, value in zip(coefficients, values):
        if value is None:
            continue
        term = float(coefficient) * value
        total = term if total is None else total + term
    return total


def line_product(matrix, line, sign):
    pairs = [(line[k], line[6 - k]) for k in range(3)]
    even = [None if a is None else a + b for a, b in pairs] + [line[3]]
    odd = [None if a is None else a - b for a, b in pairs]
    out = [None] * 7
    for i in range(3):
        even_row = [0.5 * (matrix[i, k] + matrix[i, 6 - k]) for k in range(3)] + [matrix[i, 3]]
        odd_row = [0.5 * (matrix[i, k] - matrix[i, 6 - k]) for k in range(3)]
        even_part = weighted_sum(even_row, even)
        odd_part = weighted_sum(odd_row, odd)
        out[i] = even_part + odd_part
        out[6 - i] = even_part - odd_part if sign > 0 else odd_part - even_part
    if sign > 0:
        out[3] = weighted_sum([matrix[3, k] for k in range(4)], even)
    else:
        out[3] = weighted_sum([matrix[3, k] for k in range(3)], odd)
    return out


def kernel(
    mesh_x,
    mesh_z,
    vel_hbm,
    slot_hbm,
    table_hbm,
    out,
    vel,
    slot,
    table,
    msg,
    recv1,
    phys,
    span,
    cross,
    send2,
    recv2,
    basis,
    last_faces,
    edge_tile,
    edge_recv,
    moments,
    halo_send,
    halo_recv,
    red_x,
    red_z,
    send1_sem,
    recv1_sem,
    own1_sem,
    send2_sem,
    recv2_sem,
    own2_sem,
    halo_send_sem,
    halo_recv_sem,
    redx_send_sem,
    redx_recv_sem,
    redz_send_sem,
    redz_recv_sem,
    load_sem,
    edge_send_sem,
    edge_recv_sem,
):
    def vel_load(f):
        part = pl.ds(f * PLANES_PER_FIELD, PLANES_PER_FIELD)
        return pltpu.make_async_copy(vel_hbm.at[part], vel.at[part], load_sem.at[f])

    slot_load = pltpu.make_async_copy(slot_hbm, slot, load_sem.at[FIELDS])
    table_load = pltpu.make_async_copy(table_hbm, table, load_sem.at[FIELDS + 1])
    slot_load.start()
    for f in range(FIELDS):
        vel_load(f).start()
    table_load.start()

    me = lax.axis_index("modes")
    strip = lax.axis_index("mesh")
    strips = mesh_x * mesh_z
    at_x = lax.rem(strip, mesh_x)
    at_z = strip // mesh_x
    following = lax.rem(strip + 1, strips)
    previous = lax.rem(strip + strips - 1, strips)

    def mode_peer(step):
        return lax.rem(me + step, GROUPS)

    def x_peer(step):
        return at_z * mesh_x + lax.rem(at_x + step, mesh_x)

    def z_peer(step):
        return lax.rem(at_z + step, mesh_z) * mesh_x + at_x

    barrier = pltpu.get_barrier_semaphore()
    greeted = [{"modes": mode_peer(step)} for step in range(1, GROUPS)]
    greeted += [{"mesh": following}, {"mesh": previous}]
    greeted += [{"mesh": x_peer(step)} for step in range(1, mesh_x)]
    greeted += [{"mesh": z_peer(step)} for step in range(1, mesh_z)]
    greeted += [{"modes": 0, "mesh": following}, {"modes": GROUPS - 1, "mesh": previous}]
    greetings = len(greeted) - 2
    greetings += jnp.where(jnp.logical_or(me == 0, me == GROUPS - 1), GROUPS, 0)
    for device in greeted:
        pl.semaphore_signal(
            barrier, inc=1, device_id=device, device_id_type=pl.DeviceIdType.MESH
        )

    lane = lax.broadcasted_iota(jnp.int32, (8, LANES), 1)
    group = lane // EY
    row = lane % EY
    slot_load.wait()
    slots = jnp.broadcast_to(slot[...], (8, LANES))

    def remote(src, dst, send, recv, device):
        return pltpu.make_async_remote_copy(
            src_ref=src,
            dst_ref=dst,
            send_sem=send,
            recv_sem=recv,
            device_id=device,
            device_id_type=pl.DeviceIdType.MESH,
        )

    def out_copy(f, step):
        peer = mode_peer(step)
        part = pl.ds(*OUT_PARTS[f])
        return remote(
            msg.at[peer, part],
            recv1.at[part, pl.ds(me * LOCAL, LOCAL)],
            send1_sem.at[f, step - 1],
            recv1_sem.at[f, step - 1],
            {"modes": peer},
        )

    def own_out(f):
        part = pl.ds(*OUT_PARTS[f])
        return pltpu.make_async_copy(
            msg.at[me, part], recv1.at[part, pl.ds(me * LOCAL, LOCAL)], own1_sem.at[f]
        )

    def back_copy(f, step):
        peer = mode_peer(step)
        part = pl.ds(*BACK_PARTS[f])
        return remote(
            send2.at[part, pl.ds(peer * LOCAL, LOCAL)],
            recv2.at[me, part],
            send2_sem.at[f, step - 1],
            recv2_sem.at[f, step - 1],
            {"modes": peer},
        )

    def own_back(f):
        part = pl.ds(*BACK_PARTS[f])
        return pltpu.make_async_copy(
            send2.at[part, pl.ds(me * LOCAL, LOCAL)], recv2.at[me, part], own2_sem.at[f]
        )

    def edge_copy(side, f, owner):
        return remote(
            (edge_tile if side == 0 else send2).at[
                f if side == 0 else f * 6, pl.ds(pl.multiple_of(owner * LOCAL, LOCAL), LOCAL)
            ],
            edge_recv.at[side, f],
            edge_send_sem.at[side, f, owner],
            edge_recv_sem.at[side, f],
            {"modes": owner, "mesh": following if side == 0 else previous},
        )

    def for_edges(action):
        for side, worker in ((0, GROUPS - 1), (1, 0)):

            @pl.when(me == worker)
            def _(side=side):
                def each(owner, carry):
                    action(side, owner)
                    return carry

                lax.fori_loop(0, GROUPS, each, 0)

    def halo_copies(level):
        return (
            remote(
                halo_send.at[level, 0],
                halo_recv.at[level, 0],
                halo_send_sem.at[level, 0],
                halo_recv_sem.at[level, 0],
                {"mesh": following},
            ),
            remote(
                halo_send.at[level, 1],
                halo_recv.at[level, 1],
                halo_send_sem.at[level, 1],
                halo_recv_sem.at[level, 1],
                {"mesh": previous},
            ),
        )

    def pack_faces(level, f, rows, lefts, rights):
        to_next = pltpu.roll(rights[0], EY, 1)
        to_prior = lefts[0]
        for j in range(1, NODES):
            here = group == j
            right = pltpu.roll(rights[j], EY * (j + 1), 1)
            to_next = jnp.where(here, right, to_next)
            to_prior = jnp.where(here, pltpu.roll(lefts[j], EY * j, 1), to_prior)
        halo_send[level, 0, f, rows, :] = to_next
        halo_send[level, 1, f, rows, :] = to_prior

    def order_line(f, i):
        for half in range(2):
            rows = pl.ds(8 * half, 8)
            for j in range(NODES):
                at = f * PLANES_PER_FIELD + i * NODES + j
                vel[at, rows, :] = jnp.take_along_axis(vel[at, rows, :], slots, axis=1)

    def spread_line(f, i):
        for half in range(2):
            rows = pl.ds(8 * half, 8)
            base = f * PLANES_PER_FIELD
            tiles = [vel[base + i * NODES + j, rows, :] for j in range(NODES)]
            tiles = swap_groups(tiles + [vel[base + 42 + i, rows, :]], group)
            for k in range(GROUPS):
                msg[k, 1 + f * 6 + i, rows, :] = tiles[k]

    for f in range(FIELDS):
        vel_load(f).wait()
        order_line(f, 6)
    for half in range(2):
        rows = pl.ds(8 * half, 8)
        zero = jnp.zeros((8, LANES), jnp.float32)
        tiles = [vel[f * PLANES_PER_FIELD + 48, rows, :] for f in range(FIELDS)]
        tiles = swap_groups(tiles + [zero] * 5, group)
        for k in range(GROUPS):
            msg[k, 0, rows, :] = tiles[k]
    for f in range(FIELDS):

        def one_line(i, carry, f=f):
            order_line(f, i)
            spread_line(f, i)
            return carry

        lax.fori_loop(0, NODES - 1, one_line, 0)
        if f == 0:
            pl.semaphore_wait(barrier, greetings)
        for step in range(1, GROUPS):
            out_copy(f, step).start()
        own_out(f).start()

    for f in range(FIELDS):
        base = f * PLANES_PER_FIELD
        for half in range(2):
            rows = pl.ds(8 * half, 8)
            lefts = [vel[base + j, rows, :] for j in range(NODES)]
            rights = [vel[base + 42 + j, rows, :] for j in range(NODES)]
            pack_faces(0, f, rows, lefts, rights)
    for copy in halo_copies(0):
        copy.start()

    table_load.wait()
    tt, tl, bb = table.at[0:256, :], table.at[256:512, 0:128], table.at[256:512, 128:256]
    ff, fl, bl = table.at[512:640, :], table.at[640:768, 0:128], table.at[640:768, 128:256]
    group_all = lax.broadcasted_iota(jnp.int32, (NCOEF, LANES), 1) // EY

    def shifted(value, slots_up):
        return pltpu.roll(value, (EY * slots_up) % LANES, 1) if slots_up % GROUPS else value

    for f in range(FIELDS):
        for step in range(1, GROUPS):
            out_copy(f, step).wait_recv()
        own_out(f).wait()
        last = jnp.where(group_all == 6, shifted(recv1[0], 6 - f), 0.0)
        for i in range(6):
            last = jnp.where(group_all == i, shifted(recv1[1 + f * 6 + i], i - 7), last)
        for i in range(NODES):
            at = f * NODES + i
            high, low = split_value(recv1[1 + f * 6 + i] if i < 6 else last)
            value = dot(tt[...], jnp.concatenate([high, low], axis=0)) + dot(tl[...], high)
            planes = value[:NCOEF]
            phys[at] = planes
            span[at] = value[NCOEF:]
            high, low = split_value(planes)
            cross[at] = dot(jnp.concatenate([high, low], axis=1), bb[...]) + dot(high, bl[...])

    rest = jnp.zeros((NCOEF, LANES), jnp.float32)
    for f in range(FIELDS):

        def rows_of(block, inner, f=f):
            rows = pl.ds(pl.multiple_of(block * 8, 8), 8)
            line = [phys[f * NODES + i, rows, :] for i in range(NODES)]
            stream = line_product(2.0 * DERIV, line, -1)
            for i in range(NODES):
                at = f * NODES + i
                cross[at, rows, :] = (
                    phys[i, rows, :] * stream[i]
                    + phys[NODES + i, rows, :] * cross[at, rows, :]
                    + phys[2 * NODES + i, rows, :] * span[at, rows, :]
                )
            return inner

        lax.fori_loop(0, NCOEF // 8, rows_of, 0)
        for i in (6, 0, 1, 2, 3, 4, 5):
            high, low = split_value(cross[f * NODES + i])
            value = dot(ff[...], jnp.concatenate([high, low], axis=0)) + dot(fl[...], high)
            if i == 6:
                last = value
                edge_tile[f] = value
                rest = jnp.where(group_all == f, shifted(value, f - 6), rest)
            else:
                send2[f * 6 + i] = jnp.where(group_all == 7, shifted(last, 7 - i), value)
        if f == FIELDS - 1:
            send2[TILES - 1] = rest
        for_edges(lambda side, owner, f=f: edge_copy(side, f, owner).start())
        for step in range(1, GROUPS):
            back_copy(f, step).start()
        own_back(f).start()

    is_first = strip == 0
    is_last = strip == strips - 1
    not_inflow = jnp.logical_not(jnp.logical_and(group == 0, is_first))
    west = group == 0
    east = group == GROUPS - 1
    south = row != 0
    north = row != EY - 1
    has_previous = jnp.where(is_first, 0.0, 1.0)
    has_following = jnp.where(is_last, 0.0, 1.0)
    east_weight = jnp.where(jnp.logical_and(east, is_last), 1.0, 0.5)

    def at_block(block):
        f = block // 2
        rows = pl.ds(pl.multiple_of((block % 2) * 8, 8), 8)
        return f, rows

    def over_blocks(body, first=0, last=2 * FIELDS):
        lax.fori_loop(first, last, lambda block, c: (body(block), c)[1], 0, unroll=2)

    def gather_source(f):
        for step in range(1, GROUPS):
            back_copy(f, step).wait_recv()
        own_back(f).wait()
        base = f * PLANES_PER_FIELD
        for half in range(2):
            rows = pl.ds(8 * half, 8)
            for i in range(6):
                tiles = swap_groups([recv2[k, f * 6 + i, rows, :] for k in range(GROUPS)], group)
                for j in range(8):
                    a, b = (i, j) if j < 7 else (6, i)
                    at = base + a * NODES + b
                    basis[0, at, rows, :] = float(MASS[a, b]) * (
                        SIGMA_BASE * vel[at, rows, :] + tiles[j]
                    )

    def gather_rest():
        for half in range(2):
            rows = pl.ds(8 * half, 8)
            tiles = swap_groups([recv2[k, TILES - 1, rows, :] for k in range(GROUPS)], group)
            for f in range(FIELDS):
                at = f * PLANES_PER_FIELD + 48
                basis[0, at, rows, :] = float(MASS[6, 6]) * (
                    SIGMA_BASE * vel[at, rows, :] + tiles[f]
                )

    def along_rows(line):
        bottom, top = line[0], line[6]
        first = jnp.where(south, bottom + pltpu.roll(top, 1, 1), 0.0)
        last = jnp.where(north, top + pltpu.roll(bottom, LANES - 1, 1), 0.0)
        return [first] + list(line[1:6]) + [last]

    def squares(line):
        total = line[1] * line[1]
        for j in range(2, 6):
            total = total + line[j] * line[j]
        return total + 0.5 * (line[0] * line[0] + line[6] * line[6])

    def shift_of(block):
        number = (
            me * LOCAL + (block % 2) * 8 + lax.broadcasted_iota(jnp.int32, (8, LANES), 0)
        )
        wave = jnp.where(number <= NCOEF // 2, number, number - NCOEF // 2).astype(jnp.float32)
        wave = SPAN_WAVE * wave
        return 0.25 * (SIGMA_BASE + wave * wave)

    def finish_inside(level, first=0, last=2 * FIELDS):
        def block_of(block):
            f, rows = at_block(block)
            base = f * PLANES_PER_FIELD
            shift = shift_of(block)
            total = jnp.zeros((8, LANES), jnp.float32)
            inside = []
            for i in range(1, 6):
                line = []
                for j in range(NODES):
                    value = basis[level, base + i * NODES + j, rows, :]
                    if level:
                        value = float(QUAD[i] * QUAD[j]) * (
                            value
                            + float(SCALED_STIFF[i, 0]) * basis[level - 1, base + j, rows, :]
                            + float(SCALED_STIFF[i, 6]) * basis[level - 1, base + 42 + j, rows, :]
                        )
                    line.append(value)
                line = along_rows(line)
                for j in range(NODES):
                    if level or j in (0, 6):
                        basis[level, base + i * NODES + j, rows, :] = line[j]
                total = total + squares(line)
                inside.append(line)
            image = [None] * PLANES_PER_FIELD
            for j in range(NODES):
                column = [None] + [line[j] for line in inside] + [None]
                column = line_product(SCALED_STIFF, column, 1)
                for i in range(NODES):
                    image[i * NODES + j] = column[i]
            energy = jnp.zeros((8, LANES), jnp.float32)
            for i in range(1, 6):
                line = line_product(SCALED_STIFF, inside[i - 1], 1)
                for j in range(NODES):
                    n = i * NODES + j
                    image[n] = image[n] + line[j] + shift * inside[i - 1][j]
                    energy = energy + float(QUAD[i] * QUAD[j]) * (image[n] * inside[i - 1][j])
            for n in range(PLANES_PER_FIELD):
                if level < 2:
                    basis[level + 1, base + n, rows, :] = image[n]
                elif n < 7:
                    last_faces[0, f, n, rows, :] = image[n]
                elif n >= 42:
                    last_faces[1, f, n - 42, rows, :] = image[n]
            moments[2 * level, f, rows, :] = total
            moments[2 * level + 1, f, rows, :] = energy

        over_blocks(block_of, first, last)

    def finish_faces(level):
        def block_of(block):
            f, rows = at_block(block)
            base = f * PLANES_PER_FIELD
            shift = shift_of(block)
            prior = halo_recv[level, 0, f, rows, :]
            after = halo_recv[level, 1, f, rows, :]
            if level == 0:
                prior = SIGMA_BASE * prior + edge_recv[0, f, rows, :]
                after = SIGMA_BASE * after + edge_recv[1, f, rows, :]
            prior = prior * has_previous
            after = after * has_following
            lefts, rights = [], []
            for j in range(NODES):
                left = basis[level, base + j, rows, :]
                right = basis[level, base + 42 + j, rows, :]
                from_prior = pltpu.roll(prior, LANES - EY * j, 1) if j else prior
                from_after = pltpu.roll(after, LANES - EY * (j + 1), 1)
                if level == 0:
                    from_prior = float(MASS[6, j]) * from_prior
                    from_after = float(MASS[0, j]) * from_after
                lefts.append(left + jnp.where(west, from_prior, pltpu.roll(right, EY, 1)))
                rights.append(
                    right + jnp.where(east, from_after, pltpu.roll(left, LANES - EY, 1))
                )
            lefts = [jnp.where(not_inflow, value, 0.0) for value in along_rows(lefts)]
            rights = along_rows(rights)
            moments[2 * level, f, rows, :] = (
                moments[2 * level, f, rows, :]
                + 0.5 * squares(lefts)
                + east_weight * squares(rights)
            )
            energy = moments[2 * level + 1, f, rows, :]
            images = []
            for i, line in ((0, lefts), (6, rights)):
                across = line_product(SCALED_STIFF, line, 1)
                image = []
                for j in range(NODES):
                    basis[level, base + i * NODES + j, rows, :] = line[j]
                    if level < 2:
                        part = basis[level + 1, base + i * NODES + j, rows, :]
                    else:
                        part = last_faces[i // 6, f, j, rows, :]
                    whole = (
                        part
                        + float(SCALED_STIFF[i, 0]) * lefts[j]
                        + float(SCALED_STIFF[i, 6]) * rights[j]
                        + across[j]
                        + shift * line[j]
                    )
                    weight = float(QUAD[i] * QUAD[j])
                    energy = energy + weight * ((whole + part) * line[j])
                    if level < 2:
                        whole = weight * whole
                        basis[level + 1, base + i * NODES + j, rows, :] = whole
                        image.append(whole)
                images.append(image)
            moments[2 * level + 1, f, rows, :] = energy
            if level < 2:
                pack_faces(level + 1, f, rows, images[0], images[1])

        over_blocks(block_of)

    def pack_moments(packed, which):
        for m in which:
            for block in range(2 * FIELDS):
                f, half = block // 2, block % 2
                total = jnp.sum(moments[m, f, 8 * half : 8 * half + 8, :], axis=1, keepdims=True)
                packed = jnp.where(lane == 8 * block + m, total, packed)
        return packed

    packed = jnp.zeros((8, LANES), jnp.float32)
    for level in range(3):
        if level == 0:
            for f in range(FIELDS):
                gather_source(f)
                finish_inside(0, 2 * f, 2 * f + 2)
                for side in range(2):
                    edge_copy(side, f, 0).wait_recv()
            gather_rest()
        else:
            finish_inside(level)
            packed = pack_moments(packed, (2 * level - 2, 2 * level - 1))
        for copy in halo_copies(level):
            copy.wait_recv()
        finish_faces(level)
        if level < 2:
            for copy in halo_copies(level + 1):
                copy.start()
    packed = pack_moments(packed, (4, 5))

    def sum_over(value, slots_ref, mine, count, copies):
        slots_ref[mine] = value
        for copy in copies:
            copy.start()
        for copy in copies:
            copy.wait_recv()
        total = slots_ref[0]
        for k in range(1, count):
            total = total + slots_ref[k]
        return total

    x_copies = [
        remote(
            red_x.at[at_x],
            red_x.at[at_x],
            redx_send_sem.at[step - 1],
            redx_recv_sem.at[step - 1],
            {"mesh": x_peer(step)},
        )
        for step in range(1, mesh_x)
    ]
    z_copies = [
        remote(
            red_z.at[at_z],
            red_z.at[at_z],
            redz_send_sem.at[step - 1],
            redz_recv_sem.at[step - 1],
            {"mesh": z_peer(step)},
        )
        for step in range(1, mesh_z)
    ]
    packed = sum_over(packed, red_x, at_x, mesh_x, x_copies)
    packed = sum_over(packed, red_z, at_z, mesh_z, z_copies)

    m0, m1, m2, m3, m4, m5 = [
        packed if m == 0 else pltpu.roll(packed, LANES - m, 1) for m in range(MOMENTS)
    ]
    s0, s1, s2 = lax.rsqrt(m1), lax.rsqrt(m3), lax.rsqrt(m5)
    l10 = m2 * s0 * s1
    l20 = m3 * s0 * s2
    h21 = m4 * s1 * s2
    d1 = 1.0 - l10 * l10
    l21 = (h21 - l20 * l10) / d1
    d2 = 1.0 - l20 * l20 - l21 * l21 * d1
    y0 = m0 * s0
    y1 = m1 * s1 - l10 * y0
    y2 = m2 * s2 - l20 * y0 - l21 * y1
    c2 = y2 / d2
    c1 = y1 / d1 - l21 * c2
    c0 = y0 - l10 * c1 - l20 * c2
    c0, c1, c2 = c0 * s0, c1 * s1, c2 * s2

    for block in range(2 * FIELDS):
        f, half = block // 2, block % 2
        rows = pl.ds(8 * half, 8)
        f0, f1, f2 = [
            jnp.broadcast_to(c[:, 8 * block : 8 * block + 1], (8, LANES)) for c in (c0, c1, c2)
        ]

        def combine(n, carry, f=f, rows=rows, f0=f0, f1=f1, f2=f2):
            at = f * PLANES_PER_FIELD + n
            out[at, rows, :] = (
                f0 * basis[0, at, rows, :] + f1 * basis[1, at, rows, :] + f2 * basis[2, at, rows, :]
            )
            return carry

        lax.fori_loop(0, PLANES_PER_FIELD, combine, 0, unroll=7)

    for f in range(FIELDS):
        for step in range(1, GROUPS):
            out_copy(f, step).wait_send()
            back_copy(f, step).wait_send()
        for_edges(lambda side, owner, f=f: edge_copy(side, f, owner).wait_send())
    for level in range(3):
        for copy in halo_copies(level):
            copy.wait_send()
    for copy in x_copies + z_copies:
        copy.wait_send()


def shards(mesh_x, mesh_z, velocity, element_slot):
    count = FIELDS * PLANES_PER_FIELD
    field = jnp.transpose(velocity, (0, 2, 3, 1, 4)).reshape(count, LOCAL, LANES)
    vmem = pl.BlockSpec(memory_space=pltpu.VMEM)
    lines = FIELDS * NODES
    f32 = jnp.float32
    dma = pltpu.SemaphoreType.DMA
    result = pl.pallas_call(
        functools.partial(kernel, mesh_x, mesh_z),
        out_shape=jax.ShapeDtypeStruct((count, LOCAL, LANES), f32),
        in_specs=[pl.BlockSpec(memory_space=pl.ANY)] * 3,
        out_specs=vmem,
        scratch_shapes=[
            pltpu.VMEM((count, LOCAL, LANES), f32),
            pltpu.VMEM((1, LANES), jnp.int32),
            pltpu.VMEM((768, 256), jnp.bfloat16),
            pltpu.VMEM((GROUPS, TILES, LOCAL, LANES), f32),
            pltpu.VMEM((TILES, NCOEF, LANES), f32),
            pltpu.VMEM((lines, NCOEF, LANES), f32),
            pltpu.VMEM((lines, NCOEF, LANES), f32),
            pltpu.VMEM((lines, NCOEF, LANES), f32),
            pltpu.VMEM((TILES, NCOEF, LANES), f32),
            pltpu.VMEM((GROUPS, TILES, LOCAL, LANES), f32),
            pltpu.VMEM((3, count, LOCAL, LANES), f32),
            pltpu.VMEM((2, FIELDS, NODES, LOCAL, LANES), f32),
            pltpu.VMEM((FIELDS, NCOEF, LANES), f32),
            pltpu.VMEM((2, FIELDS, LOCAL, LANES), f32),
            pltpu.VMEM((MOMENTS, FIELDS, LOCAL, LANES), f32),
            pltpu.VMEM((3, 2, FIELDS, LOCAL, LANES), f32),
            pltpu.VMEM((3, 2, FIELDS, LOCAL, LANES), f32),
            pltpu.VMEM((mesh_x, 8, LANES), f32),
            pltpu.VMEM((mesh_z, 8, LANES), f32),
            dma((FIELDS, GROUPS - 1)),
            dma((FIELDS, GROUPS - 1)),
            dma((FIELDS,)),
            dma((FIELDS, GROUPS - 1)),
            dma((FIELDS, GROUPS - 1)),
            dma((FIELDS,)),
            dma((3, 2)),
            dma((3, 2)),
            dma((mesh_x - 1,)),
            dma((mesh_x - 1,)),
            dma((mesh_z - 1,)),
            dma((mesh_z - 1,)),
            dma((FIELDS + 2,)),
            dma((2, FIELDS, GROUPS)),
            dma((2, FIELDS)),
        ],
        compiler_params=pltpu.CompilerParams(
            collective_id=0, has_side_effects=True, vmem_limit_bytes=40 * 1024 * 1024
        ),
    )(field, element_slot.reshape(1, LANES), jnp.asarray(transform_tables()))
    return jnp.transpose(
        result.reshape(FIELDS, NODES, NODES, LOCAL, LANES), (0, 3, 1, 2, 4)
    )


def solution(mesh):
    strips = mesh.shape["mesh"]
    mesh_x = 4 if strips % 4 == 0 else 1
    placed = (P(None, "modes", None, None, "mesh"), P("mesh"))
    return jax.shard_map(
        functools.partial(shards, mesh_x, strips // mesh_x),
        mesh=mesh,
        in_specs=placed,
        out_specs=P(None, "modes", None, None, "mesh"),
        check_vma=False,
    )
```

time: 83.6 us -> 70.2 us (0.84); the launches traced: 83.2 us -> 68.9 us
  Pallas kernels: 75.3 us -> 65 us
  local copies, waits for them, and re-layouts: 7.89 us -> 3.95 us
    pallas_call x1, Pallas kernels: 75.3 us -> 65 us  [shards(): pl.pallas_call(functools.partial(kernel, mesh_x, mesh_z), out_shape=jax.S...]
    unnamed x17 -> x7, local copies, waits for them, and re-layouts: 7.89 us -> 3.95 us
where the time goes in v2:
time: 70.2 us; the launch traced here: 68.9 us
  Pallas kernels  65 us (93%)
  local copies, waits for them, and re-layouts  3.95 us (6%)
    pallas_call x1, Pallas kernels, shards(): pl.pallas_call(functools.partial(kernel, mesh_x, mesh_z), out_shape=jax.S...  65 us
    unnamed x7, local copies, waits for them, and re-layouts  3.95 us

profile of v2, /device:TPU:4, one launch (start us, length us, event | category | flops | bytes accessed | tf_op | source)
XLA Modules:
  0.0 68.9 jit_solution(16315207440778162373)
XLA Ops:
  0.0 0.0 copy-start
  0.0 1.3 %copy-done = f32[3,16,7,7,128]{4,1,3,2,0:T(8,128)S(1)} copy-done((f32[3,16,7,7,128]{4,1,3,2,0:T(8,128)S(1)}, f32[3,16,7,7,128]{4,1,3,2,0:T(8,128)}, u32[]{:S(2)}) %copy-start) | copy-done | bytes 1204248
  1.3 0.0 copy-start.1
  1.3 1.0 %copy-done.1 = bf16[768,256]{1,0:T(8,128)(2,1)S(1)} copy-done((bf16[768,256]{1,0:T(8,128)(2,1)S(1)}, bf16[768,256]{1,0:T(8,128)(2,1)}, u32[]{:S(2)}) %copy-start.1) | copy-done | bytes 393240
  2.3 0.0 copy-start.2
  2.3 0.7 copy-done.2
  2.9 65.0 %shard_map.37 = f32[147,16,128]{2,1,0:T(8,128)S(1)} custom-call(f32[147,16,128]{2,1,0:T(8,128)S(1)} %bitcast.8, s32[1,128]{1,0:T(1,128)S(1)} %bitcast.9, bf16[768,256]{1,0:T(8,128)(2,1)S(1)} %copy-done.1), custom_call_target="tpu_custom_call" | custom-call | tf_op jit(solution)/shard_map/pallas_call | solution.py:738
  67.9 1.0 %copy.5 = f32[3,16,7,7,128]{4,1,3,2,0:T(8,128)} copy(f32[3,16,7,7,128]{4,1,3,2,0:T(8,128)S(1)} %bitcast.7) | data formatting | bytes 2408448
Async XLA Ops:
  0.0 1.3 %copy-start = (f32[3,16,7,7,128]{4,1,3,2,0:T(8,128)S(1)}, f32[3,16,7,7,128]{4,1,3,2,0:T(8,128)}, u32[]{:S(2)}) copy-start(f32[3,16,7,7,128]{4,1,3,2,0:T(8,128)} %param.3) | copy-start | bytes 3612676
  1.3 1.0 %copy-start.1 = (bf16[768,256]{1,0:T(8,128)(2,1)S(1)}, bf16[768,256]{1,0:T(8,128)(2,1)}, u32[]{:S(2)}) copy-start(bf16[768,256]{1,0:T(8,128)(2,1)} %constant.2.clone.table_hbm) | copy-start | bytes 1179652
  2.3 0.7 copy-start.2

commit v3 on v2

--- a/solution.py
+++ b/solution.py
@@ -20,9 +20,11 @@
 SPAN_WAVE = 0.25
 STEP_TIME = 0.01
 MOMENTS = 6
-TILES = 19
-OUT_PARTS = ((0, 7), (7, 6), (13, 6))
-BACK_PARTS = ((0, 6), (6, 6), (12, 7))
+HALVES = 2
+TILES = 10
+SLOT = 8
+OUT_PARTS = (((0, 4), (4, 3), (7, 3)), ((1, 3), (4, 3), (7, 3)))
+BACK_PARTS = (((0, 3), (3, 3), (6, 3)), ((0, 3), (3, 3), (6, 4)))
 
 
 def gll_tables():
@@ -80,7 +82,7 @@
     f_high, f_low = split_table(-STEP_TIME * forward)
     padded = np.zeros((8, 8))
     padded[:NODES, :NODES] = 2.0 * DERIV
-    b_high, b_low = split_table(np.kron(padded.T, np.eye(EY)))
+    b_high, b_low = split_table(np.kron(np.eye(2), np.kron(padded.T, np.eye(SLOT))))
     return np.concatenate(
         [
             np.concatenate([t_high, t_high], axis=1),
@@ -102,22 +104,22 @@
     return jnp.dot(left, right, preferred_element_type=jnp.float32)
 
 
-def swap_groups(tiles, group):
+def swap_groups(tiles, lane):
     tiles = list(tiles)
-    for bit in (4, 2, 1):
-        low = (group & bit) == 0
+    for bit in (8, 4, 2, 1):
+        low = (lane & (SLOT * bit)) == 0
         new = list(tiles)
-        for at in range(8):
+        for at in range(16):
             if at & bit:
                 continue
             first, second = tiles[at], tiles[at + bit]
-            if bit == 4:
+            if bit == 8:
                 moved = pltpu.roll(jnp.where(low, second, first), 64, 1)
                 new[at] = jnp.where(low, first, moved)
                 new[at + bit] = jnp.where(low, moved, second)
             else:
-                new[at] = jnp.where(low, first, pltpu.roll(second, EY * bit, 1))
-                new[at + bit] = jnp.where(low, pltpu.roll(first, LANES - EY * bit, 1), second)
+                new[at] = jnp.where(low, first, pltpu.roll(second, SLOT * bit, 1))
+                new[at + bit] = jnp.where(low, pltpu.roll(first, LANES - SLOT * bit, 1), second)
         tiles = new
     return tiles
 
@@ -151,13 +153,29 @@
     return out
 
 
+class Levels:
+    def __init__(self, *buffers):
+        self.buffers = buffers
+
+    def __getitem__(self, at):
+        return self.buffers[at[0]][at[1:]]
+
+    def __setitem__(self, at, value):
+        self.buffers[at[0]][at[1:]] = value
+
+
 def kernel(
     mesh_x,
     mesh_z,
     vel_hbm,
     slot_hbm,
     table_hbm,
-    out,
+    basis0,
+    basis1,
+    basis2,
+    factor0,
+    factor1,
+    factor2,
     vel,
     slot,
     table,
@@ -168,7 +186,6 @@
     cross,
     send2,
     recv2,
-    basis,
     last_faces,
     edge_tile,
     edge_recv,
@@ -204,6 +221,8 @@
         vel_load(f).start()
     table_load.start()
 
+    basis = Levels(basis0, basis1, basis2)
+    factor = Levels(factor0, factor1, factor2)
     me = lax.axis_index("modes")
     strip = lax.axis_index("mesh")
     strips = mesh_x * mesh_z
@@ -250,45 +269,48 @@
             device_id_type=pl.DeviceIdType.MESH,
         )
 
-    def out_copy(f, step):
+    def out_copy(h, f, step):
         peer = mode_peer(step)
-        part = pl.ds(*OUT_PARTS[f])
+        part = pl.ds(*OUT_PARTS[h][f])
         return remote(
-            msg.at[peer, part],
-            recv1.at[part, pl.ds(me * LOCAL, LOCAL)],
-            send1_sem.at[f, step - 1],
-            recv1_sem.at[f, step - 1],
+            msg.at[h, peer, part],
+            recv1.at[h, part, pl.ds(me * LOCAL, LOCAL)],
+            send1_sem.at[h, f, step - 1],
+            recv1_sem.at[h, f, step - 1],
             {"modes": peer},
         )
 
-    def own_out(f):
-        part = pl.ds(*OUT_PARTS[f])
+    def own_out(h, f):
+        part = pl.ds(*OUT_PARTS[h][f])
         return pltpu.make_async_copy(
-            msg.at[me, part], recv1.at[part, pl.ds(me * LOCAL, LOCAL)], own1_sem.at[f]
-        )
-
-    def back_copy(f, step):
+            msg.at[h, me, part], recv1.at[h, part, pl.ds(me * LOCAL, LOCAL)], own1_sem.at[h, f]
+        )
+
+    def start_out(h, f):
+        for step in range(1, GROUPS):
+            out_copy(h, f, step).start()
+        own_out(h, f).start()
+
+    def back_copy(h, f, step):
         peer = mode_peer(step)
-        part = pl.ds(*BACK_PARTS[f])
+        part = pl.ds(*BACK_PARTS[h][f])
         return remote(
-            send2.at[part, pl.ds(peer * LOCAL, LOCAL)],
-            recv2.at[me, part],
-            send2_sem.at[f, step - 1],
-            recv2_sem.at[f, step - 1],
+            send2.at[h, part, pl.ds(peer * LOCAL, LOCAL)],
+            recv2.at[h, me, part],
+            send2_sem.at[h, f, step - 1],
+            recv2_sem.at[h, f, step - 1],
             {"modes": peer},
         )
 
-    def own_back(f):
-        part = pl.ds(*BACK_PARTS[f])
+    def own_back(h, f):
+        part = pl.ds(*BACK_PARTS[h][f])
         return pltpu.make_async_copy(
-            send2.at[part, pl.ds(me * LOCAL, LOCAL)], recv2.at[me, part], own2_sem.at[f]
+            send2.at[h, part, pl.ds(me * LOCAL, LOCAL)], recv2.at[h, me, part], own2_sem.at[h, f]
         )
 
     def edge_copy(side, f, owner):
         return remote(
-            (edge_tile if side == 0 else send2).at[
-                f if side == 0 else f * 6, pl.ds(pl.multiple_of(owner * LOCAL, LOCAL), LOCAL)
-            ],
+            edge_tile.at[side, f, pl.ds(pl.multiple_of(owner * LOCAL, LOCAL), LOCAL)],
             edge_recv.at[side, f],
             edge_send_sem.at[side, f, owner],
             edge_recv_sem.at[side, f],
@@ -342,14 +364,21 @@
                 at = f * PLANES_PER_FIELD + i * NODES + j
                 vel[at, rows, :] = jnp.take_along_axis(vel[at, rows, :], slots, axis=1)
 
-    def spread_line(f, i):
+    def store_message(tiles, at, rows):
+        tiles = swap_groups(tiles, lane)
+        for k in range(GROUPS):
+            for h in range(HALVES):
+                msg[h, k, at, rows, :] = tiles[2 * k + h]
+
+    def spread_lines(f, p):
+        base = f * PLANES_PER_FIELD
         for half in range(2):
             rows = pl.ds(8 * half, 8)
-            base = f * PLANES_PER_FIELD
-            tiles = [vel[base + i * NODES + j, rows, :] for j in range(NODES)]
-            tiles = swap_groups(tiles + [vel[base + 42 + i, rows, :]], group)
-            for k in range(GROUPS):
-                msg[k, 1 + f * 6 + i, rows, :] = tiles[k]
+            tiles = []
+            for i in (2 * p, 2 * p + 1):
+                tiles += [vel[base + i * NODES + j, rows, :] for j in range(NODES)]
+                tiles.append(vel[base + 42 + i, rows, :])
+            store_message(tiles, 1 + f * 3 + p, rows)
 
     for f in range(FIELDS):
         vel_load(f).wait()
@@ -358,22 +387,21 @@
         rows = pl.ds(8 * half, 8)
         zero = jnp.zeros((8, LANES), jnp.float32)
         tiles = [vel[f * PLANES_PER_FIELD + 48, rows, :] for f in range(FIELDS)]
-        tiles = swap_groups(tiles + [zero] * 5, group)
+        tiles = swap_groups(tiles + [zero] * 13, lane)
         for k in range(GROUPS):
-            msg[k, 0, rows, :] = tiles[k]
+            msg[0, k, 0, rows, :] = tiles[2 * k] + pltpu.roll(tiles[2 * k + 1], 3 * SLOT, 1)
     for f in range(FIELDS):
 
-        def one_line(i, carry, f=f):
-            order_line(f, i)
-            spread_line(f, i)
+        def two_lines(p, carry, f=f):
+            order_line(f, 2 * p)
+            order_line(f, 2 * p + 1)
+            spread_lines(f, p)
             return carry
 
-        lax.fori_loop(0, NODES - 1, one_line, 0)
+        lax.fori_loop(0, 3, two_lines, 0)
         if f == 0:
             pl.semaphore_wait(barrier, greetings)
-        for step in range(1, GROUPS):
-            out_copy(f, step).start()
-        own_out(f).start()
+        start_out(0, f)
 
     for f in range(FIELDS):
         base = f * PLANES_PER_FIELD
@@ -388,60 +416,99 @@
     table_load.wait()
     tt, tl, bb = table.at[0:256, :], table.at[256:512, 0:128], table.at[256:512, 128:256]
     ff, fl, bl = table.at[512:640, :], table.at[640:768, 0:128], table.at[640:768, 128:256]
-    group_all = lax.broadcasted_iota(jnp.int32, (NCOEF, LANES), 1) // EY
+    slot_all = lax.broadcasted_iota(jnp.int32, (NCOEF, LANES), 1) // SLOT
+    low_half = lane < 64
 
     def shifted(value, slots_up):
-        return pltpu.roll(value, (EY * slots_up) % LANES, 1) if slots_up % GROUPS else value
-
-    for f in range(FIELDS):
-        for step in range(1, GROUPS):
-            out_copy(f, step).wait_recv()
-        own_out(f).wait()
-        last = jnp.where(group_all == 6, shifted(recv1[0], 6 - f), 0.0)
-        for i in range(6):
-            last = jnp.where(group_all == i, shifted(recv1[1 + f * 6 + i], i - 7), last)
-        for i in range(NODES):
-            at = f * NODES + i
-            high, low = split_value(recv1[1 + f * 6 + i] if i < 6 else last)
+        return pltpu.roll(value, (SLOT * slots_up) % LANES, 1) if slots_up % 16 else value
+
+    def to_planes(h, f):
+        tiles = [recv1[h, 1 + 3 * f + p] for p in range(3)]
+        last = jnp.where(slot_all == 6, shifted(recv1[0, 0], 6 - f - 3 * h), 0.0)
+        for j in range(6):
+            last = jnp.where(
+                slot_all == j, shifted(tiles[j // 2], j - 7 - 8 * (j % 2)), last
+            )
+        tiles.append(last)
+        planes = []
+        for p in (0, 2):
+            high, low = split_value(jnp.concatenate(tiles[p : p + 2], axis=1))
             value = dot(tt[...], jnp.concatenate([high, low], axis=0)) + dot(tl[...], high)
-            planes = value[:NCOEF]
-            phys[at] = planes
-            span[at] = value[NCOEF:]
-            high, low = split_value(planes)
-            cross[at] = dot(jnp.concatenate([high, low], axis=1), bb[...]) + dot(high, bl[...])
-
-    rest = jnp.zeros((NCOEF, LANES), jnp.float32)
-    for f in range(FIELDS):
-
-        def rows_of(block, inner, f=f):
+            for q in range(2):
+                at = 4 * f + p + q
+                planes.append(value[:NCOEF, q * LANES : (q + 1) * LANES])
+                phys[at] = planes[-1]
+                span[at] = value[NCOEF:, q * LANES : (q + 1) * LANES]
+        high, low = split_value(jnp.concatenate(planes, axis=0))
+        value = dot(jnp.concatenate([high, low], axis=1), bb[...]) + dot(high, bl[...])
+        for p in range(4):
+            cross[4 * f + p] = value[p * NCOEF : (p + 1) * NCOEF]
+
+    def derivative_at(i, a):
+        return float(2.0 * DERIV[i, a]) if i < NODES and a < NODES else 0.0
+
+    def advect(h, f):
+        def rows_of(block, inner):
             rows = pl.ds(pl.multiple_of(block * 8, 8), 8)
-            line = [phys[f * NODES + i, rows, :] for i in range(NODES)]
-            stream = line_product(2.0 * DERIV, line, -1)
-            for i in range(NODES):
-                at = f * NODES + i
+            tiles = [phys[4 * f + p, rows, :] for p in range(4)]
+            swapped = [pltpu.roll(tile, 64, 1) for tile in tiles]
+            both = tiles[3] + swapped[3]
+            for p in range(4):
+                i = 2 * p
+                stream = both * jnp.where(low_half, derivative_at(i, 6), derivative_at(i + 1, 6))
+                for q in range(3):
+                    a = 2 * q
+                    stream = (
+                        stream
+                        + tiles[q]
+                        * jnp.where(low_half, derivative_at(i, a), derivative_at(i + 1, a + 1))
+                        + swapped[q]
+                        * jnp.where(low_half, derivative_at(i, a + 1), derivative_at(i + 1, a))
+                    )
+                at = 4 * f + p
                 cross[at, rows, :] = (
-                    phys[i, rows, :] * stream[i]
-                    + phys[NODES + i, rows, :] * cross[at, rows, :]
-                    + phys[2 * NODES + i, rows, :] * span[at, rows, :]
+                    phys[p, rows, :] * stream
+                    + phys[4 + p, rows, :] * cross[at, rows, :]
+                    + phys[8 + p, rows, :] * span[at, rows, :]
                 )
             return inner
 
-        lax.fori_loop(0, NCOEF // 8, rows_of, 0)
-        for i in (6, 0, 1, 2, 3, 4, 5):
-            high, low = split_value(cross[f * NODES + i])
+        lax.fori_loop(0, NCOEF // 8, rows_of, 0, unroll=2)
+        last = None
+        for p in (2, 0):
+            pair = jnp.concatenate([cross[4 * f + p], cross[4 * f + p + 1]], axis=1)
+            high, low = split_value(pair)
             value = dot(ff[...], jnp.concatenate([high, low], axis=0)) + dot(fl[...], high)
-            if i == 6:
-                last = value
-                edge_tile[f] = value
-                rest = jnp.where(group_all == f, shifted(value, f - 6), rest)
-            else:
-                send2[f * 6 + i] = jnp.where(group_all == 7, shifted(last, 7 - i), value)
-        if f == FIELDS - 1:
-            send2[TILES - 1] = rest
-        for_edges(lambda side, owner, f=f: edge_copy(side, f, owner).start())
+            parts = [value[:, :LANES], value[:, LANES:]]
+            if p == 2:
+                last = parts.pop()
+            for q, part in reversed(list(enumerate(parts))):
+                i = 2 * (p + q)
+                part = jnp.where(slot_all == 7, shifted(last, 7 - i), part)
+                send2[h, 3 * f + p + q] = jnp.where(slot_all == 15, shifted(last, 14 - i), part)
+        at = 3 * h + f
+        rest = send2[1, TILES - 1] if at else jnp.zeros((NCOEF, LANES), jnp.float32)
+        send2[1, TILES - 1] = jnp.where(slot_all == at, shifted(last, at - 6), rest)
+        for side, tile in ((0, last), (1, part)):
+            if h:
+                tile = jnp.where(slot_all < 8, edge_tile[side, f], shifted(tile, 8))
+            edge_tile[side, f] = tile
+        if h:
+            for_edges(lambda side, owner: edge_copy(side, f, owner).start())
         for step in range(1, GROUPS):
-            back_copy(f, step).start()
-        own_back(f).start()
+            back_copy(h, f, step).start()
+        own_back(h, f).start()
+
+    for h in range(HALVES):
+        for f in range(FIELDS):
+            for step in range(1, GROUPS):
+                out_copy(h, f, step).wait_recv()
+            own_out(h, f).wait()
+            if h == 0:
+                start_out(1, f)
+            to_planes(h, f)
+        for f in range(FIELDS):
+            advect(h, f)
 
     is_first = strip == 0
     is_last = strip == strips - 1
@@ -459,29 +526,37 @@
         rows = pl.ds(pl.multiple_of((block % 2) * 8, 8), 8)
         return f, rows
 
-    def over_blocks(body, first=0, last=2 * FIELDS):
-        lax.fori_loop(first, last, lambda block, c: (body(block), c)[1], 0, unroll=2)
+    def over_blocks(body, first=0, last=2 * FIELDS, unroll=2):
+        lax.fori_loop(first, last, lambda block, c: (body(block), c)[1], 0, unroll=unroll)
 
     def gather_source(f):
-        for step in range(1, GROUPS):
-            back_copy(f, step).wait_recv()
-        own_back(f).wait()
+        for h in range(HALVES):
+            for step in range(1, GROUPS):
+                back_copy(h, f, step).wait_recv()
+            own_back(h, f).wait()
         base = f * PLANES_PER_FIELD
         for half in range(2):
             rows = pl.ds(8 * half, 8)
-            for i in range(6):
-                tiles = swap_groups([recv2[k, f * 6 + i, rows, :] for k in range(GROUPS)], group)
-                for j in range(8):
+            for p in range(3):
+                tiles = swap_groups(
+                    [recv2[g % 2, g // 2, 3 * f + p, rows, :] for g in range(16)], lane
+                )
+                for s in range(16):
+                    i, j = 2 * p + s // 8, s % 8
                     a, b = (i, j) if j < 7 else (6, i)
                     at = base + a * NODES + b
                     basis[0, at, rows, :] = float(MASS[a, b]) * (
-                        SIGMA_BASE * vel[at, rows, :] + tiles[j]
+                        SIGMA_BASE * vel[at, rows, :] + tiles[s]
                     )
 
     def gather_rest():
         for half in range(2):
             rows = pl.ds(8 * half, 8)
-            tiles = swap_groups([recv2[k, TILES - 1, rows, :] for k in range(GROUPS)], group)
+            tiles = []
+            for k in range(GROUPS):
+                tile = recv2[1, k, TILES - 1, rows, :]
+                tiles += [tile, shifted(tile, -3)]
+            tiles = swap_groups(tiles, lane)
             for f in range(FIELDS):
                 at = f * PLANES_PER_FIELD + 48
                 basis[0, at, rows, :] = float(MASS[6, 6]) * (
@@ -565,8 +640,10 @@
             prior = halo_recv[level, 0, f, rows, :]
             after = halo_recv[level, 1, f, rows, :]
             if level == 0:
-                prior = SIGMA_BASE * prior + edge_recv[0, f, rows, :]
-                after = SIGMA_BASE * after + edge_recv[1, f, rows, :]
+                prior = SIGMA_BASE * prior
+                after = SIGMA_BASE * after
+                prior_edge = edge_recv[0, f, rows, :] * has_previous
+                after_edge = edge_recv[1, f, rows, :] * has_following
             prior = prior * has_previous
             after = after * has_following
             lefts, rights = [], []
@@ -576,8 +653,18 @@
                 from_prior = pltpu.roll(prior, LANES - EY * j, 1) if j else prior
                 from_after = pltpu.roll(after, LANES - EY * (j + 1), 1)
                 if level == 0:
-                    from_prior = float(MASS[6, j]) * from_prior
-                    from_after = float(MASS[0, j]) * from_after
+                    from_prior = float(MASS[6, j]) * (
+                        from_prior
+                        + jnp.where(
+                            lane < 8, shifted(prior_edge, -j), shifted(prior_edge, -7 - j)
+                        )
+                    )
+                    from_after = float(MASS[0, j]) * (
+                        from_after
+                        + jnp.where(
+                            lane < 120, shifted(after_edge, 14 - j), shifted(after_edge, 7 - j)
+                        )
+                    )
                 lefts.append(left + jnp.where(west, from_prior, pltpu.roll(right, EY, 1)))
                 rights.append(
                     right + jnp.where(east, from_after, pltpu.roll(left, LANES - EY, 1))
@@ -618,7 +705,7 @@
             if level < 2:
                 pack_faces(level + 1, f, rows, images[0], images[1])
 
-        over_blocks(block_of)
+        over_blocks(block_of, unroll=6)
 
     def pack_moments(packed, which):
         for m in which:
@@ -702,24 +789,17 @@
 
     for block in range(2 * FIELDS):
         f, half = block // 2, block % 2
-        rows = pl.ds(8 * half, 8)
-        f0, f1, f2 = [
-            jnp.broadcast_to(c[:, 8 * block : 8 * block + 1], (8, LANES)) for c in (c0, c1, c2)
-        ]
-
-        def combine(n, carry, f=f, rows=rows, f0=f0, f1=f1, f2=f2):
-            at = f * PLANES_PER_FIELD + n
-            out[at, rows, :] = (
-                f0 * basis[0, at, rows, :] + f1 * basis[1, at, rows, :] + f2 * basis[2, at, rows, :]
+        for k, c in enumerate((c0, c1, c2)):
+            factor[k, f, 8 * half : 8 * half + 8, :] = jnp.broadcast_to(
+                c[:, 8 * block : 8 * block + 1], (8, LANES)
             )
-            return carry
-
-        lax.fori_loop(0, PLANES_PER_FIELD, combine, 0, unroll=7)
-
+
+    for h in range(HALVES):
+        for f in range(FIELDS):
+            for step in range(1, GROUPS):
+                out_copy(h, f, step).wait_send()
+                back_copy(h, f, step).wait_send()
     for f in range(FIELDS):
-        for step in range(1, GROUPS):
-            out_copy(f, step).wait_send()
-            back_copy(f, step).wait_send()
         for_edges(lambda side, owner, f=f: edge_copy(side, f, owner).wait_send())
     for level in range(3):
         for copy in halo_copies(level):
@@ -732,40 +812,45 @@
     count = FIELDS * PLANES_PER_FIELD
     field = jnp.transpose(velocity, (0, 2, 3, 1, 4)).reshape(count, LOCAL, LANES)
     vmem = pl.BlockSpec(memory_space=pltpu.VMEM)
-    lines = FIELDS * NODES
     f32 = jnp.float32
     dma = pltpu.SemaphoreType.DMA
-    result = pl.pallas_call(
+    *basis, factor0, factor1, factor2 = pl.pallas_call(
         functools.partial(kernel, mesh_x, mesh_z),
-        out_shape=jax.ShapeDtypeStruct((count, LOCAL, LANES), f32),
-        in_specs=[pl.BlockSpec(memory_space=pl.ANY)] * 3,
-        out_specs=vmem,
+        out_shape=[
+            jax.ShapeDtypeStruct((count, LOCAL, LANES), f32),
+        ]
+        * 3
+        + [
+            jax.ShapeDtypeStruct((FIELDS, LOCAL, LANES), f32),
+        ]
+        * 3,
+        in_specs=[pl.BlockSpec(memory_space=pltpu.HBM)] * 3,
+        out_specs=[vmem] * 6,
         scratch_shapes=[
             pltpu.VMEM((count, LOCAL, LANES), f32),
             pltpu.VMEM((1, LANES), jnp.int32),
             pltpu.VMEM((768, 256), jnp.bfloat16),
-            pltpu.VMEM((GROUPS, TILES, LOCAL, LANES), f32),
-            pltpu.VMEM((TILES, NCOEF, LANES), f32),
-            pltpu.VMEM((lines, NCOEF, LANES), f32),
-            pltpu.VMEM((lines, NCOEF, LANES), f32),
-            pltpu.VMEM((lines, NCOEF, LANES), f32),
-            pltpu.VMEM((TILES, NCOEF, LANES), f32),
-            pltpu.VMEM((GROUPS, TILES, LOCAL, LANES), f32),
-            pltpu.VMEM((3, count, LOCAL, LANES), f32),
+            pltpu.VMEM((HALVES, GROUPS, TILES, LOCAL, LANES), f32),
+            pltpu.VMEM((HALVES, TILES, NCOEF, LANES), f32),
+            pltpu.VMEM((4 * FIELDS, NCOEF, LANES), f32),
+            pltpu.VMEM((4 * FIELDS, NCOEF, LANES), f32),
+            pltpu.VMEM((4 * FIELDS, NCOEF, LANES), f32),
+            pltpu.VMEM((HALVES, TILES, NCOEF, LANES), f32),
+            pltpu.VMEM((HALVES, GROUPS, TILES, LOCAL, LANES), f32),
             pltpu.VMEM((2, FIELDS, NODES, LOCAL, LANES), f32),
-            pltpu.VMEM((FIELDS, NCOEF, LANES), f32),
+            pltpu.VMEM((2, FIELDS, NCOEF, LANES), f32),
             pltpu.VMEM((2, FIELDS, LOCAL, LANES), f32),
             pltpu.VMEM((MOMENTS, FIELDS, LOCAL, LANES), f32),
             pltpu.VMEM((3, 2, FIELDS, LOCAL, LANES), f32),
             pltpu.VMEM((3, 2, FIELDS, LOCAL, LANES), f32),
             pltpu.VMEM((mesh_x, 8, LANES), f32),
             pltpu.VMEM((mesh_z, 8, LANES), f32),
-            dma((FIELDS, GROUPS - 1)),
-            dma((FIELDS, GROUPS - 1)),
-            dma((FIELDS,)),
-            dma((FIELDS, GROUPS - 1)),
-            dma((FIELDS, GROUPS - 1)),
-            dma((FIELDS,)),
+            dma((HALVES, FIELDS, GROUPS - 1)),
+            dma((HALVES, FIELDS, GROUPS - 1)),
+            dma((HALVES, FIELDS)),
+            dma((HALVES, FIELDS, GROUPS - 1)),
+            dma((HALVES, FIELDS, GROUPS - 1)),
+            dma((HALVES, FIELDS)),
             dma((3, 2)),
             dma((3, 2)),
             dma((mesh_x - 1,)),
@@ -777,12 +862,15 @@
             dma((2, FIELDS)),
         ],
         compiler_params=pltpu.CompilerParams(
-            collective_id=0, has_side_effects=True, vmem_limit_bytes=40 * 1024 * 1024
+            collective_id=0, has_side_effects=True, vmem_limit_bytes=50688 * 1024
         ),
     )(field, element_slot.reshape(1, LANES), jnp.asarray(transform_tables()))
-    return jnp.transpose(
-        result.reshape(FIELDS, NODES, NODES, LOCAL, LANES), (0, 3, 1, 2, 4)
-    )
+    terms = [
+        factor[:, None, None] * level.reshape(FIELDS, NODES, NODES, LOCAL, LANES)
+        for level, factor in zip(basis, (factor0, factor1, factor2))
+    ]
+    result = terms[0] + terms[1] + terms[2]
+    return jnp.transpose(result, (0, 3, 1, 2, 4))
 
 
 def solution(mesh):

time: 70.2 us -> 63.9 us (0.910)
  Pallas kernels: 65 us -> 59.9 us
  local copies, waits for them, and re-layouts: 3.95 us -> 1.65 us
  other arithmetic: 0 us -> 1.36 us
    pallas_call x1, Pallas kernels: 65 us -> 59.9 us  [shards(): pl.pallas_call(functools.partial(kernel, mesh_x, mesh_z), out_shape=[jax....]
    unnamed x7 -> x4, local copies, waits for them, and re-layouts: 3.95 us -> 1.65 us
    transpose x0 -> x1, other arithmetic: none -> 1.36 us  [shards(): return jnp.transpose(result, (0, 3, 1, 2, 4))]
where the time goes in v3:
time: 63.9 us; the launch traced here: 62.9 us
  Pallas kernels  59.9 us (94%)
  local copies, waits for them, and re-layouts  1.65 us (3%)
  other arithmetic  1.36 us (2%)
    pallas_call x1, Pallas kernels, shards(): pl.pallas_call(functools.partial(kernel, mesh_x, mesh_z), out_shape=[jax....  59.9 us
    unnamed x4, local copies, waits for them, and re-layouts  1.65 us
    transpose x1, other arithmetic, shards(): return jnp.transpose(result, (0, 3, 1, 2, 4))  1.36 us

profile of v3, /device:TPU:4, one launch (start us, length us, event | category | flops | bytes accessed | tf_op | source)
XLA Modules:
  0.0 62.9 jit_solution(14450238354626355983)
XLA Ops:
  0.0 0.0 copy-start
  0.0 1.0 %copy-done = bf16[768,256]{1,0:T(8,128)(2,1)S(1)} copy-done((bf16[768,256]{1,0:T(8,128)(2,1)S(1)}, bf16[768,256]{1,0:T(8,128)(2,1)}, u32[]{:S(2)}) %copy-start) | copy-done | bytes 393240
  1.0 0.0 copy-start.1
  1.0 0.7 %copy-done.1 = s32[128]{0:T(128)S(1)} copy-done((s32[128]{0:T(128)S(1)}, s32[128]{0:T(128)}, u32[]{:S(2)}) %copy-start.1) | copy-done | bytes 536
  1.7 59.9 %shard_map.37 = (f32[147,16,128]{2,1,0:T(8,128)S(1)}, f32[147,16,128]{2,1,0:T(8,128)S(1)}, f32[147,16,128]{2,1,0:T(8,128)S(1)}, f32[3,16,128]{2,1,0:T(8,128)S(1)...) custom-call(f32[147,16,128]{2,1,0:T(8,128)} %bitcast.13, s32[1,128]{1,0:T(1,128)S(1)} %bitcast.12, ...), custom_call_target="tpu_custom_call" | custom-call | tf_op jit(solution)/shard_map/pallas_call | solution.py:817
  61.6 1.4 %add_bitcast_fusion = f32[3,16,7,7,128]{4,1,3,2,0:T(8,128)} fusion(f32[3,7,7,16,128]{4,3,2,1,0:T(8,128)S(1)} %bitcast.11, f32[3,7,7,16,128]{4,3,2,1,0:T(8,128)S(1)} %bitcast.10, f32[3,7,7,16,128]{4,3,2,1,0:T(8,128)S(1)} %bitcast.9, f32[3,16,128]{2,1,0:T(8,128)S(1)} %get-tuple-element.15, f32[3,16,128]{2,1,0:T(8,128)S(1)} %get-tuple-element.13, ...), kind=kLoop, calls=%fused_computation | loop fusion | flops 1505280 | bytes 4890624 | tf_op jit(solution)/shard_map/transpose | solution.py:873
Async XLA Ops:
  0.0 1.0 %copy-start = (bf16[768,256]{1,0:T(8,128)(2,1)S(1)}, bf16[768,256]{1,0:T(8,128)(2,1)}, u32[]{:S(2)}) copy-start(bf16[768,256]{1,0:T(8,128)(2,1)} %constant.2.clone.table_hbm) | copy-start | bytes 1179652
  1.0 0.7 %copy-start.1 = (s32[128]{0:T(128)S(1)}, s32[128]{0:T(128)}, u32[]{:S(2)}) copy-start(s32[128]{0:T(128)} %param.4) | copy-start | bytes 1540

commit v4 on v3

--- a/solution.py
+++ b/solution.py
@@ -20,6 +20,8 @@
 SPAN_WAVE = 0.25
 STEP_TIME = 0.01
 MOMENTS = 6
+TABLE_ROWS = 768
+TABLE_HELD = 4096
 HALVES = 2
 TILES = 10
 SLOT = 8
@@ -89,6 +91,7 @@
             np.concatenate([t_low, np.concatenate([b_high, b_high], axis=0)], axis=1),
             np.concatenate([f_high, f_high], axis=1),
             np.concatenate([f_low, b_low], axis=1),
+            np.zeros((TABLE_HELD - TABLE_ROWS, 256), jnp.bfloat16),
         ],
         axis=0,
     )
@@ -187,6 +190,7 @@
     send2,
     recv2,
     last_faces,
+    beside,
     edge_tile,
     edge_recv,
     moments,
@@ -215,7 +219,9 @@
         return pltpu.make_async_copy(vel_hbm.at[part], vel.at[part], load_sem.at[f])
 
     slot_load = pltpu.make_async_copy(slot_hbm, slot, load_sem.at[FIELDS])
-    table_load = pltpu.make_async_copy(table_hbm, table, load_sem.at[FIELDS + 1])
+    table_load = pltpu.make_async_copy(
+        table_hbm.at[0:TABLE_ROWS], table, load_sem.at[FIELDS + 1]
+    )
     slot_load.start()
     for f in range(FIELDS):
         vel_load(f).start()
@@ -629,8 +635,25 @@
                     last_faces[1, f, n - 42, rows, :] = image[n]
             moments[2 * level, f, rows, :] = total
             moments[2 * level + 1, f, rows, :] = energy
-
-        over_blocks(block_of, first, last)
+            if level == 1:
+                lefts = [basis[1, base + j, rows, :] for j in range(NODES)]
+                rights = [basis[1, base + 42 + j, rows, :] for j in range(NODES)]
+                inner_rights = along_rows(
+                    [b + pltpu.roll(a, LANES - EY, 1) for a, b in zip(lefts, rights)]
+                )
+                inner_lefts = along_rows([a + pltpu.roll(b, EY, 1) for a, b in zip(lefts, rights)])
+                pack_faces(
+                    2,
+                    f,
+                    rows,
+                    [image[j] + float(SCALED_STIFF[0, 6]) * inner_rights[j] for j in range(NODES)],
+                    [
+                        image[42 + j] + float(SCALED_STIFF[6, 0]) * inner_lefts[j]
+                        for j in range(NODES)
+                    ],
+                )
+
+        over_blocks(block_of, first, last, unroll=6 if last - first > 2 else 2)
 
     def finish_faces(level):
         def block_of(block):
@@ -665,6 +688,10 @@
                             lane < 120, shifted(after_edge, 14 - j), shifted(after_edge, 7 - j)
                         )
                     )
+                if level == 2:
+                    weight = float(QUAD[0] * QUAD[j])
+                    from_prior = weight * (from_prior + beside[0, f, j, rows, :])
+                    from_after = weight * (from_after + beside[1, f, j, rows, :])
                 lefts.append(left + jnp.where(west, from_prior, pltpu.roll(right, EY, 1)))
                 rights.append(
                     right + jnp.where(east, from_after, pltpu.roll(left, LANES - EY, 1))
@@ -694,6 +721,11 @@
                         + across[j]
                         + shift * line[j]
                     )
+                    if level == 1:
+                        has_side = has_previous if i == 0 else has_following
+                        beside[i // 6, f, j, rows, :] = has_side * (
+                            float(SCALED_STIFF[0, 0]) * line[j] + across[j] + shift * line[j]
+                        )
                     weight = float(QUAD[i] * QUAD[j])
                     energy = energy + weight * ((whole + part) * line[j])
                     if level < 2:
@@ -702,10 +734,19 @@
                         image.append(whole)
                 images.append(image)
             moments[2 * level + 1, f, rows, :] = energy
-            if level < 2:
-                pack_faces(level + 1, f, rows, images[0], images[1])
+            if level == 0:
+                pack_faces(1, f, rows, images[0], images[1])
 
         over_blocks(block_of, unroll=6)
+
+    def wait_sent():
+        for h in range(HALVES):
+            for f in range(FIELDS):
+                for step in range(1, GROUPS):
+                    out_copy(h, f, step).wait_send()
+                    back_copy(h, f, step).wait_send()
+        for f in range(FIELDS):
+            for_edges(lambda side, owner, f=f: edge_copy(side, f, owner).wait_send())
 
     def pack_moments(packed, which):
         for m in which:
@@ -726,12 +767,17 @@
             gather_rest()
         else:
             finish_inside(level)
+            if level == 1:
+                for copy in halo_copies(2):
+                    copy.start()
             packed = pack_moments(packed, (2 * level - 2, 2 * level - 1))
+            if level == 1:
+                wait_sent()
         for copy in halo_copies(level):
             copy.wait_recv()
         finish_faces(level)
-        if level < 2:
-            for copy in halo_copies(level + 1):
+        if level == 0:
+            for copy in halo_copies(1):
                 copy.start()
     packed = pack_moments(packed, (4, 5))
 
@@ -794,13 +840,6 @@
                 c[:, 8 * block : 8 * block + 1], (8, LANES)
             )
 
-    for h in range(HALVES):
-        for f in range(FIELDS):
-            for step in range(1, GROUPS):
-                out_copy(h, f, step).wait_send()
-                back_copy(h, f, step).wait_send()
-    for f in range(FIELDS):
-        for_edges(lambda side, owner, f=f: edge_copy(side, f, owner).wait_send())
     for level in range(3):
         for copy in halo_copies(level):
             copy.wait_send()
@@ -829,7 +868,7 @@
         scratch_shapes=[
             pltpu.VMEM((count, LOCAL, LANES), f32),
             pltpu.VMEM((1, LANES), jnp.int32),
-            pltpu.VMEM((768, 256), jnp.bfloat16),
+            pltpu.VMEM((TABLE_ROWS, 256), jnp.bfloat16),
             pltpu.VMEM((HALVES, GROUPS, TILES, LOCAL, LANES), f32),
             pltpu.VMEM((HALVES, TILES, NCOEF, LANES), f32),
             pltpu.VMEM((4 * FIELDS, NCOEF, LANES), f32),
@@ -837,6 +876,7 @@
             pltpu.VMEM((4 * FIELDS, NCOEF, LANES), f32),
             pltpu.VMEM((HALVES, TILES, NCOEF, LANES), f32),
             pltpu.VMEM((HALVES, GROUPS, TILES, LOCAL, LANES), f32),
+            pltpu.VMEM((2, FIELDS, NODES, LOCAL, LANES), f32),
             pltpu.VMEM((2, FIELDS, NODES, LOCAL, LANES), f32),
             pltpu.VMEM((2, FIELDS, NCOEF, LANES), f32),
             pltpu.VMEM((2, FIELDS, LOCAL, LANES), f32),

time: 63.9 us -> 59.4 us (0.930); the launches traced: 62.9 us -> 59.3 us
  Pallas kernels: 59.9 us -> 57.3 us
  local copies, waits for them, and re-layouts: 1.65 us -> 0.65 us
    pallas_call x1, Pallas kernels: 59.9 us -> 57.3 us  [shards(): pl.pallas_call(functools.partial(kernel, mesh_x, mesh_z), out_shape=[jax....]
    unnamed x4 -> x2, local copies, waits for them, and re-layouts: 1.65 us -> 0.65 us
where the time goes in v4:
time: 59.4 us; the launch traced here: 59.3 us
  Pallas kernels  57.3 us (96%)
  other arithmetic  1.36 us (2%)
  local copies, waits for them, and re-layouts  0.65 us (1%)
    pallas_call x1, Pallas kernels, shards(): pl.pallas_call(functools.partial(kernel, mesh_x, mesh_z), out_shape=[jax....  57.3 us
    transpose x1, other arithmetic, shards(): return jnp.transpose(result, (0, 3, 1, 2, 4))  1.36 us

profile of v4, /device:TPU:4, one launch (start us, length us, event | category | flops | bytes accessed | tf_op | source)
XLA Modules:
  0.0 59.3 jit_solution(11803141960258277280)
XLA Ops:
  0.0 0.0 copy-start
  0.0 0.7 %copy-done = s32[128]{0:T(128)S(1)} copy-done((s32[128]{0:T(128)S(1)}, s32[128]{0:T(128)}, u32[]{:S(2)}) %copy-start) | copy-done | bytes 536
  0.7 57.3 %shard_map.37 = (f32[147,16,128]{2,1,0:T(8,128)S(1)}, f32[147,16,128]{2,1,0:T(8,128)S(1)}, f32[147,16,128]{2,1,0:T(8,128)S(1)}, f32[3,16,128]{2,1,0:T(8,128)S(1)...) custom-call(f32[147,16,128]{2,1,0:T(8,128)} %bitcast.13, s32[1,128]{1,0:T(1,128)S(1)} %bitcast.12, ...), custom_call_target="tpu_custom_call" | custom-call | tf_op jit(solution)/shard_map/pallas_call | solution.py:856
  58.0 1.4 %add_bitcast_fusion = f32[3,16,7,7,128]{4,1,3,2,0:T(8,128)} fusion(f32[3,7,7,16,128]{4,3,2,1,0:T(8,128)S(1)} %bitcast.11, f32[3,7,7,16,128]{4,3,2,1,0:T(8,128)S(1)} %bitcast.10, f32[3,7,7,16,128]{4,3,2,1,0:T(8,128)S(1)} %bitcast.9, f32[3,16,128]{2,1,0:T(8,128)S(1)} %get-tuple-element.15, f32[3,16,128]{2,1,0:T(8,128)S(1)} %get-tuple-element.13, ...), kind=kLoop, calls=%fused_computation | loop fusion | flops 1505280 | bytes 4890624 | tf_op jit(solution)/shard_map/transpose | solution.py:913
Async XLA Ops:
  0.0 0.7 %copy-start = (s32[128]{0:T(128)S(1)}, s32[128]{0:T(128)}, u32[]{:S(2)}) copy-start(s32[128]{0:T(128)} %param.4) | copy-start | bytes 1540

commit v5 on v4

--- a/solution.py
+++ b/solution.py
@@ -222,11 +222,6 @@
     table_load = pltpu.make_async_copy(
         table_hbm.at[0:TABLE_ROWS], table, load_sem.at[FIELDS + 1]
     )
-    slot_load.start()
-    for f in range(FIELDS):
-        vel_load(f).start()
-    table_load.start()
-
     basis = Levels(basis0, basis1, basis2)
     factor = Levels(factor0, factor1, factor2)
     me = lax.axis_index("modes")
@@ -258,6 +253,11 @@
         pl.semaphore_signal(
             barrier, inc=1, device_id=device, device_id_type=pl.DeviceIdType.MESH
         )
+
+    slot_load.start()
+    for f in range(FIELDS):
+        vel_load(f).start()
+    table_load.start()
 
     lane = lax.broadcasted_iota(jnp.int32, (8, LANES), 1)
     group = lane // EY
@@ -812,8 +812,8 @@
         )
         for step in range(1, mesh_z)
     ]
+    packed = sum_over(packed, red_z, at_z, mesh_z, z_copies)
     packed = sum_over(packed, red_x, at_x, mesh_x, x_copies)
-    packed = sum_over(packed, red_z, at_z, mesh_z, z_copies)
 
     m0, m1, m2, m3, m4, m5 = [
         packed if m == 0 else pltpu.roll(packed, LANES - m, 1) for m in range(MOMENTS)

time: 59.4 us -> 59.4 us (level)
  no operation moved by 1% of the time
where the time goes in v5:
time: 59.4 us; the launch traced here: 59.3 us
  Pallas kernels  57.2 us (96%)
  other arithmetic  1.36 us (2%)
  local copies, waits for them, and re-layouts  0.65 us (1%)
    pallas_call x1, Pallas kernels, shards(): pl.pallas_call(functools.partial(kernel, mesh_x, mesh_z), out_shape=[jax....  57.2 us
    transpose x1, other arithmetic, shards(): return jnp.transpose(result, (0, 3, 1, 2, 4))  1.36 us

profile of v5, /device:TPU:4, one launch (start us, length us, event | category | flops | bytes accessed | tf_op | source)
XLA Modules:
  0.0 59.3 jit_solution(13881227812421914068)
XLA Ops:
  0.0 0.0 copy-start
  0.0 0.7 %copy-done = s32[128]{0:T(128)S(1)} copy-done((s32[128]{0:T(128)S(1)}, s32[128]{0:T(128)}, u32[]{:S(2)}) %copy-start) | copy-done | bytes 536
  0.7 57.2 %shard_map.37 = (f32[147,16,128]{2,1,0:T(8,128)S(1)}, f32[147,16,128]{2,1,0:T(8,128)S(1)}, f32[147,16,128]{2,1,0:T(8,128)S(1)}, f32[3,16,128]{2,1,0:T(8,128)S(1)...) custom-call(f32[147,16,128]{2,1,0:T(8,128)} %bitcast.13, s32[1,128]{1,0:T(1,128)S(1)} %bitcast.12, ...), custom_call_target="tpu_custom_call" | custom-call | tf_op jit(solution)/shard_map/pallas_call | solution.py:856
  57.9 1.4 %add_bitcast_fusion = f32[3,16,7,7,128]{4,1,3,2,0:T(8,128)} fusion(f32[3,7,7,16,128]{4,3,2,1,0:T(8,128)S(1)} %bitcast.11, f32[3,7,7,16,128]{4,3,2,1,0:T(8,128)S(1)} %bitcast.10, f32[3,7,7,16,128]{4,3,2,1,0:T(8,128)S(1)} %bitcast.9, f32[3,16,128]{2,1,0:T(8,128)S(1)} %get-tuple-element.15, f32[3,16,128]{2,1,0:T(8,128)S(1)} %get-tuple-element.13, ...), kind=kLoop, calls=%fused_computation | loop fusion | flops 1505280 | bytes 4890624 | tf_op jit(solution)/shard_map/transpose | solution.py:913
Async XLA Ops:
  0.0 0.7 %copy-start = (s32[128]{0:T(128)S(1)}, s32[128]{0:T(128)}, u32[]{:S(2)}) copy-start(s32[128]{0:T(128)} %param.4) | copy-start | bytes 1540

commit v6 on v5

--- a/solution.py
+++ b/solution.py
@@ -386,7 +386,19 @@
                 tiles.append(vel[base + 42 + i, rows, :])
             store_message(tiles, 1 + f * 3 + p, rows)
 
-    for f in range(FIELDS):
+    def spread_field(f):
+        def two_lines(p, carry):
+            order_line(f, 2 * p)
+            order_line(f, 2 * p + 1)
+            spread_lines(f, p)
+            return carry
+
+        lax.fori_loop(0, 3, two_lines, 0)
+
+    vel_load(0).wait()
+    order_line(0, 6)
+    spread_field(0)
+    for f in range(1, FIELDS):
         vel_load(f).wait()
         order_line(f, 6)
     for half in range(2):
@@ -396,17 +408,10 @@
         tiles = swap_groups(tiles + [zero] * 13, lane)
         for k in range(GROUPS):
             msg[0, k, 0, rows, :] = tiles[2 * k] + pltpu.roll(tiles[2 * k + 1], 3 * SLOT, 1)
+    pl.semaphore_wait(barrier, greetings)
     for f in range(FIELDS):
-
-        def two_lines(p, carry, f=f):
-            order_line(f, 2 * p)
-            order_line(f, 2 * p + 1)
-            spread_lines(f, p)
-            return carry
-
-        lax.fori_loop(0, 3, two_lines, 0)
-        if f == 0:
-            pl.semaphore_wait(barrier, greetings)
+        if f:
+            spread_field(f)
         start_out(0, f)
 
     for f in range(FIELDS):

time: 59.4 us -> 59.4 us (level)
  no operation moved by 1% of the time
where the time goes in v6:
time: 59.4 us; the launch traced here: 59.3 us
  Pallas kernels  57.2 us (96%)
  other arithmetic  1.36 us (2%)
  local copies, waits for them, and re-layouts  0.65 us (1%)
    pallas_call x1, Pallas kernels, shards(): pl.pallas_call(functools.partial(kernel, mesh_x, mesh_z), out_shape=[jax....  57.2 us
    transpose x1, other arithmetic, shards(): return jnp.transpose(result, (0, 3, 1, 2, 4))  1.36 us

profile of v6, /device:TPU:4, one launch (start us, length us, event | category | flops | bytes accessed | tf_op | source)
XLA Modules:
  0.0 59.3 jit_solution(8429124172568429271)
XLA Ops:
  0.0 0.0 copy-start
  0.0 0.7 %copy-done = s32[128]{0:T(128)S(1)} copy-done((s32[128]{0:T(128)S(1)}, s32[128]{0:T(128)}, u32[]{:S(2)}) %copy-start) | copy-done | bytes 536
  0.7 57.2 %shard_map.37 = (f32[147,16,128]{2,1,0:T(8,128)S(1)}, f32[147,16,128]{2,1,0:T(8,128)S(1)}, f32[147,16,128]{2,1,0:T(8,128)S(1)}, f32[3,16,128]{2,1,0:T(8,128)S(1)...) custom-call(f32[147,16,128]{2,1,0:T(8,128)} %bitcast.13, s32[1,128]{1,0:T(1,128)S(1)} %bitcast.12, ...), custom_call_target="tpu_custom_call" | custom-call | tf_op jit(solution)/shard_map/pallas_call | solution.py:861
  57.9 1.4 %add_bitcast_fusion = f32[3,16,7,7,128]{4,1,3,2,0:T(8,128)} fusion(f32[3,7,7,16,128]{4,3,2,1,0:T(8,128)S(1)} %bitcast.11, f32[3,7,7,16,128]{4,3,2,1,0:T(8,128)S(1)} %bitcast.10, f32[3,7,7,16,128]{4,3,2,1,0:T(8,128)S(1)} %bitcast.9, f32[3,16,128]{2,1,0:T(8,128)S(1)} %get-tuple-element.15, f32[3,16,128]{2,1,0:T(8,128)S(1)} %get-tuple-element.13, ...), kind=kLoop, calls=%fused_computation | loop fusion | flops 1505280 | bytes 4890624 | tf_op jit(solution)/shard_map/transpose | solution.py:918
Async XLA Ops:
  0.0 0.7 %copy-start = (s32[128]{0:T(128)S(1)}, s32[128]{0:T(128)}, u32[]{:S(2)}) copy-start(s32[128]{0:T(128)} %param.4) | copy-start | bytes 1540
